TPU v7x, 1024 devices: a whole 4x8x16 slice. The times are simulated.
1024 devices in a mesh: row: 16 (over x, z_lo), col: 64 (over y, z_hi, core).
Axes of the slice: x: 4, y: 8, z: 16 (z_hi: 4, z_lo: 4; z = z_hi * 4 + z_lo), core: 2. Of those that a mesh axis runs over, the one named last changes fastest.
Arguments:
- gradient: float32 [8192, 28672], P('row', 'col'), may hold values from -6 to 6
- weight: float32 [8192, 28672], P('row', 'col'), may hold values from -6 to 6
- projector: float32 [8192, 512], P('row', 'col'), may hold values from -0.0625 to 0.0625
- first_moment: float32 [512, 28672], P(None, 'col'), may hold values from -4 to 4
- second_moment: float32 [512, 28672], P(None, 'col'), may hold values from 0.01 to 1
Outputs:
- new_first: float32 [512, 28672], P(None, 'col')
- new_second: float32 [512, 28672], P(None, 'col')
- update: float32 [8192, 28672], P('row', 'col')
All inputs are finite; a program needn't handle non-finite values.
Results may differ from a plain program's by a relative error of at most 0.00007.
Values sent between devices are 32-bit elements; how exact they have to be, the bound alone decides.
No kernel may reach another device: no remote copies, remote signals or barrier semaphores. Data moves between devices by JAX's collectives and lax.ppermute only.
A program may use at most 32 MiB of HBM per device.

v0:
```python
import jax
import jax.numpy as jnp
from jax import lax
from jax.sharding import PartitionSpec as P

STEP = 100


def adam_step(low, first_moment, second_moment):
    new_first = 0.9 * first_moment + 0.1 * low
    new_second = 0.999 * second_moment + 0.001 * low * low
    corr_one = 1.0 - 0.9**STEP
    corr_two = 1.0 - 0.999**STEP
    normed = new_first / corr_one / (jnp.sqrt(new_second / corr_two) + 1e-08)
    return (new_first, new_second, normed)


def body(gradient, weight, projector, first_moment, second_moment):
    full_proj = lax.all_gather(projector, "col", axis=1, tiled=True)
    rank_all = full_proj.shape[1]
    share_rows = rank_all // lax.axis_size("row")
    reduced = lax.psum_scatter(
        jnp.dot(
            full_proj.T,
            gradient,
            precision=lax.Precision.HIGHEST,
            preferred_element_type=jnp.float32,
        ),
        "row",
        scatter_dimension=0,
        tiled=True,
    )
    offset = lax.axis_index("row") * share_rows
    old_first = lax.dynamic_slice_in_dim(first_moment, offset, share_rows, 0)
    old_second = lax.dynamic_slice_in_dim(second_moment, offset, share_rows, 0)
    part_first, part_second, normed = adam_step(reduced, old_first, old_second)
    total = jnp.dot(
        full_proj,
        lax.all_gather(normed, "row", axis=0, tiled=True),
        precision=lax.Precision.HIGHEST,
        preferred_element_type=jnp.float32,
    )
    moment_one = lax.all_gather(part_first, "row", axis=0, tiled=True)
    moment_two = lax.all_gather(part_second, "row", axis=0, tiled=True)
    update = 0.25 * total + 0.1 * weight
    return (moment_one, moment_two, update)


def solution(mesh):
    return jax.shard_map(
        body,
        mesh=mesh,
        in_specs=(
            P("row", "col"),
            P("row", "col"),
            P("row", "col"),
            P(None, "col"),
            P(None, "col"),
        ),
        out_specs=(P(None, "col"), P(None, "col"), P("row", "col")),
        check_vma=False,
    )
```

profile of v0, /device:TPU:32, one launch (start us, length us, event | category | flops | bytes accessed | tf_op | source)
XLA Modules:
  0.0 375.4 jit_solution(8702182668069350894)
XLA Ops:
  7.2 0.0 copy-start
  7.2 0.0 all-gather.2.cloned.1.call-start
  7.2 0.7 all-gather.2.cloned.1.call-update
  7.9 0.0 reduce-scatter.2.cloned.1.call-start
  8.0 109.3 %all-gather.2.cloned.1.call-done = f32[512,512]{0,1:T(8,128)} async-done(((f32[512,8]{0,1:T(8,128)}), f32[512,512]{0,1:T(8,128)}) %all-gather.2.cloned.1.call-update) | async-done | bytes 1048592 | tf_op jit(solution)/shard_map/all_gather | solution.py:19
  117.2 0.0 copy-done
  117.2 4.1 %fusion.4 = f32[512,448]{1,0:T(8,128)} fusion(f32[512,512]{0,1:T(8,128)} %all-gather.2.cloned.1.call-done, f32[512,448]{0,1:T(8,128)S(1)} %copy-done), kind=kOutput, calls=%fused_computation.9 | convolution fusion | flops 1409286144 | bytes 2883584 | tf_op jit(solution)/shard_map/dot_general | solution.py:23
  121.3 0.0 reduce-scatter.2.cloned.1.call-update
  121.3 1.2 constant_dynamic-slice_fusion
  122.6 0.1 copy.13
  122.7 0.1 copy.12
  122.8 89.8 %reduce-scatter.2.cloned.1.call-done = f32[32,448]{1,0:T(8,128)} async-done(((f32[512,448]{1,0:T(8,128)}), f32[32,448]{1,0:T(8,128)}) %reduce-scatter.2.cloned.1.call-update) | async-done | bytes 57360 | tf_op jit(solution)/shard_map/reduce_scatter | solution.py:22
  212.6 0.9 add_divide_fusion
  213.5 49.0 %all_gather.15 = f32[512,448]{1,0:T(8,128)} all-gather(f32[32,448]{1,0:T(8,128)S(1)} %get-tuple-element.6), channel_id=1, replica_groups=mesh['row'=16,'col'=64] {'row'}, dimensions={0}, use_global_device_ids=true | all-gather | bytes 974848 | tf_op jit(solution)/shard_map/all_gather | solution.py:39
  262.4 52.2 %all_gather.14 = f32[512,448]{1,0:T(8,128)S(1)} all-gather(f32[32,448]{1,0:T(8,128)S(1)} %get-tuple-element.7), channel_id=1, replica_groups=mesh['row'=16,'col'=64] {'row'}, dimensions={0}, use_global_device_ids=true | all-gather | bytes 974848 | tf_op jit(solution)/shard_map/all_gather | solution.py:44
  314.6 1.2 copy.11
  315.8 47.1 %all_gather.13 = f32[512,448]{1,0:T(8,128)S(1)} all-gather(f32[32,448]{1,0:T(8,128)S(1)} %get-tuple-element.8), channel_id=1, replica_groups=mesh['row'=16,'col'=64] {'row'}, dimensions={0}, use_global_device_ids=true | all-gather | bytes 974848 | tf_op jit(solution)/shard_map/all_gather | solution.py:43
  362.9 0.0 copy-start.1
  362.9 1.2 copy.10
  364.2 0.0 copy-done.1
  364.2 4.4 %fusion.1 = f32[512,448]{0,1:T(8,128)} fusion(f32[512,448]{1,0:T(8,128)} %all_gather.15, f32[512,512]{0,1:T(8,128)S(1)} %copy-done.1, f32[512,448]{0,1:T(8,128)} %param.6), kind=kOutput, calls=%fused_computation.2 | convolution fusion | flops 1409974272 | bytes 3801088 | tf_op jit(solution)/shard_map/dot_general | solution.py:37
Async XLA Ops:
  7.2 110.1 %copy-start = (f32[512,448]{0,1:T(8,128)S(1)}, f32[512,448]{0,1:T(8,128)}, u32[]{:S(2)}) copy-start(f32[512,448]{0,1:T(8,128)} %param.5) | copy-start | bytes 2752516
  7.2 110.0 %all-gather.2.cloned.1.call-start = ((), (), s32[]{:S(2)}) async-start(), calls=%async_computation.1 | async-start | bytes 1064960 | tf_op jit(solution)/shard_map/all_gather | solution.py:19
  7.9 204.7 %reduce-scatter.2.cloned.1.call-start = ((), (), s32[]{:S(2)}) async-start(), calls=%async_computation.2 | async-start | bytes 1114112 | tf_op jit(solution)/shard_map/reduce_scatter | solution.py:22
  362.9 1.2 copy-start.1
Sparse Core Ops, SparseCore 0:
  12.5 104.6 all-gather.1
  121.5 91.0 reduce-scatter.1
where the time goes:
time: 376 us; the launch traced here: 375 us
  waiting for transfers between devices  200 us (53%)
  blocking collectives  148 us (39%)
  between operations  14.1 us (4%)
  matrix products  8.5 us (2%)
  local copies, waits for them, and re-layouts  3.95 us (1%)
    all_gather x1, waiting for transfers between devices, body(): full_proj = lax.all_gather(projector, 'col', axis=1, tiled=True)  109 us
    reduce_scatter x1, waiting for transfers between devices, body(): lax.psum_scatter(jnp.dot(full_proj.T, gradient, precision=lax.Precision.H...  89.8 us
    all_gather x1, blocking collectives, body(): moment_two = lax.all_gather(part_second, 'row', axis=0, tiled=True)  52.2 us
    all_gather x1, blocking collectives, body(): lax.all_gather(normed, 'row', axis=0, tiled=True)  49 us
    all_gather x1, blocking collectives, body(): moment_one = lax.all_gather(part_first, 'row', axis=0, tiled=True)  47.1 us
  transfers between devices with their start and end apart: 2, of which 2 were waited for; matrix products, arithmetic and copies ran while one was open for 0% of the time, Pallas kernels for 0%

commit v1 on v0

v1 whole, which is shorter than its diff:
```python
import jax
import jax.numpy as jnp
from jax import lax
from jax.sharding import Mesh, PartitionSpec as P

STEP = 100
SPLIT = (("x", 4), ("zl", 4), ("y", 8), ("zh", 4), ("core", 2))
ROW = ("x", "zl")
COL = ("y", "zh", "core")


def exchange(blocks, axis):
    return lax.all_to_all(blocks, axis, 0, 0)


def gather(block, axis):
    copies = jnp.broadcast_to(block[None], (lax.axis_size(axis),) + block.shape)
    return exchange(copies, axis).reshape(-1, block.shape[-1])


def scatter_sum(array, axis):
    parts = lax.axis_size(axis)
    blocks = array.reshape(parts, array.shape[0] // parts, array.shape[1])
    return jnp.sum(exchange(blocks, axis), 0)


def dot(a, b, dims):
    return lax.dot_general(
        a, b, (dims, ((), ())),
        precision=lax.Precision.HIGH,
        preferred_element_type=jnp.float32,
    )


def body(gradient, weight, projector, first_moment, second_moment):
    ff = gradient.shape[1]
    share = projector.shape[1]
    mine = gather(gather(projector.T, "zh"), "y")
    other = lax.ppermute(mine, "core", [(0, 1), (1, 0)])
    proj = jnp.concatenate([mine, other], 0)
    rank = proj.shape[0]
    low = dot(proj, gradient, ((1,), (0,)))
    low = scatter_sum(scatter_sum(low, "x"), "zl")
    low = gather(gather(low, "zl"), "x")

    core = lax.axis_index("core")

    def swap(halves):
        return jnp.where(core == 0, halves, halves[::-1])

    low = swap(low.reshape(2, -1, share, ff)).swapaxes(0, 1).reshape(rank, ff)
    new_first = 0.9 * first_moment + 0.1 * low
    new_second = 0.999 * second_moment + 0.001 * low * low
    corr_one = 1.0 - 0.9**STEP
    corr_two = 1.0 - 0.999**STEP
    normed = new_first / corr_one / (jnp.sqrt(new_second / corr_two) + 1e-08)
    ordered = normed.reshape(-1, 2, share, ff).swapaxes(0, 1)
    ordered = swap(ordered).reshape(rank, ff)
    update = 0.25 * dot(proj, ordered, ((0,), (0,))) + 0.1 * weight
    return new_first, new_second, update


def solution(mesh):
    sizes = tuple(size for _, size in SPLIT)
    axes = tuple(name for name, _ in SPLIT)
    fine = Mesh(mesh.devices.reshape(sizes), axes)
    return jax.shard_map(
        body,
        mesh=fine,
        in_specs=(P(ROW, COL), P(ROW, COL), P(ROW, COL), P(None, COL), P(None, COL)),
        out_specs=(P(None, COL), P(None, COL), P(ROW, COL)),
        check_vma=False,
    )
```

time: 376 us -> 126 us (0.34)
  the two profiles are of different devices: /device:TPU:32 before, /device:TPU:2 now
where the time goes in v1:
time: 126 us; the launch traced here: 125 us
  blocking collectives  94 us (75%)
  waiting for transfers between devices  11.2 us (9%)
  starting transfers between devices  6.85 us (5%)
  local copies, waits for them, and re-layouts  5.73 us (5%)
  other arithmetic  3.63 us (3%)
  matrix products  3 us (2%)
    all_to_all x5, blocking collectives, exchange(): return lax.all_to_all(blocks, axis, 0, 0)  94 us
    all_to_all x1, waiting for transfers between devices, exchange(): return lax.all_to_all(blocks, axis, 0, 0)  9.36 us
    all_to_all x1, starting transfers between devices, exchange(): return lax.all_to_all(blocks, axis, 0, 0)  4.94 us
    div x1, other arithmetic, body(): normed = new_first / corr_one / (jnp.sqrt(new_second / corr_two) + 1e-08)  3.37 us
    dot_general x2, matrix products, dot(): lax.dot_general(a, b, (dims, ((), ())), precision=lax.Precision.HIGH, pre...  3 us
  transfers between devices with their start and end apart: 2, of which 2 were waited for; matrix products, arithmetic and copies ran while one was open for 0% of the time, Pallas kernels for 0%

profile of v1, /device:TPU:2, one launch (start us, length us, event | category | flops | bytes accessed | tf_op | source)
XLA Modules:
  0.0 125.2 jit_solution(3851347134617454074)
XLA Ops:
  0.6 0.0 copy-start
  0.6 0.8 broadcast_in_dim.12
  1.4 32.5 %all_to_all.30 = f32[4,8,512]{2,1,0:T(8,128)S(1)} all-to-all(f32[4,8,512]{2,1,0:T(8,128)S(1)} %broadcast_in_dim.12), channel_id=1, replica_groups=mesh['x'=4,'zl'=4,'y'=8,'zh'=4,'core'=2] {'zh'}, dimensions={0} | all-to-all | bytes 131072 | tf_op jit(solution)/shard_map/all_to_all | solution.py:13
  34.0 22.5 %all_to_all.31 = f32[8,32,512]{2,1,0:T(8,128)S(1)} all-to-all(f32[8,32,512]{2,1,0:T(8,128)S(1)} %broadcast_in_dim.28), channel_id=1, replica_groups=mesh['x'=4,'zl'=4,'y'=8,'zh'=4,'core'=2] {'y'}, dimensions={0} | all-to-all | bytes 1048576 | tf_op jit(solution)/shard_map/all_to_all | solution.py:13
  56.6 1.9 %collective-permute-start = (f32[256,512]{1,0:T(8,128)S(1)}, f32[256,512]{1,0:T(8,128)S(1)}, u32[]{:S(2)}, u32[]{:S(2)}) collective-permute-start(f32[256,512]{1,0:T(8,128)S(1)} %bitcast.21), channel_id=1, source_target_pairs={{0,1},{1,0},{2,3},{3,2},{4,5},{5,4},{6,7},{7,6},{8,9},{9,8},{10,11... | collective-permute-start | bytes 1572872 | tf_op jit(solution)/shard_map/ppermute | solution.py:39
  58.5 1.9 %collective-permute-done = f32[256,512]{1,0:T(8,128)S(1)} collective-permute-done((f32[256,512]{1,0:T(8,128)S(1)}, f32[256,512]{1,0:T(8,128)S(1)}, u32[]{:S(2)}, u32[]{:S(2)}) %collective-permute-start) | collective-permute-done | bytes 524320 | tf_op jit(solution)/shard_map/ppermute | solution.py:39
  60.4 0.0 copy-done
  60.4 0.0 copy-start.1
  60.4 0.9 convolution_bitcast_fusion
  61.3 0.0 copy-done.1
  61.3 0.1 copy.39
  61.4 17.2 %all_to_all.32 = f32[4,128,448]{1,2,0:T(8,128)S(1)} all-to-all(f32[4,128,448]{1,2,0:T(8,128)S(1)} %bitcast.29), channel_id=1, replica_groups=mesh['x'=4,'zl'=4,'y'=8,'zh'=4,'core'=2] {'x'}, dimensions={0} | all-to-all | bytes 1835008 | tf_op jit(solution)/shard_map/all_to_all | solution.py:13
  78.6 0.1 copy.25
  78.7 11.5 %all_to_all.33 = f32[4,32,448]{2,1,0:T(8,128)S(1)} all-to-all(f32[4,32,448]{2,1,0:T(8,128)S(1)} %bitcast.30), channel_id=1, replica_groups=mesh['x'=4,'zl'=4,'y'=8,'zh'=4,'core'=2] {'zl'}, dimensions={0} | all-to-all | bytes 458752 | tf_op jit(solution)/shard_map/all_to_all | solution.py:13
  90.3 10.3 %all_to_all.34 = f32[4,32,448]{2,1,0:T(8,128)S(1)} all-to-all(f32[4,32,448]{2,1,0:T(8,128)S(1)} %broadcast_in_dim.29), channel_id=1, replica_groups=mesh['x'=4,'zl'=4,'y'=8,'zh'=4,'core'=2] {'zl'}, dimensions={0} | all-to-all | bytes 458752 | tf_op jit(solution)/shard_map/all_to_all | solution.py:13
  100.5 0.1 copy.26
  100.6 1.0 broadcast_in_dim.31
  101.6 4.9 %all-to-all-start.5 = ((f32[4,128,448]{1,2,0:T(8,128)}), f32[4,128,448]{1,2,0:T(8,128)S(1)}, u32[]{:S(2)}, u32[]{:S(2)}) async-start(f32[4,128,448]{1,2,0:T(8,128)} %broadcast_in_dim.31), calls=%async_computation.5 | async-start | bytes 1835008 | tf_op jit(solution)/shard_map/all_to_all | solution.py:13
  106.6 9.4 %all-to-all-done.5 = f32[4,128,448]{1,2,0:T(8,128)S(1)} async-done(((f32[4,128,448]{1,2,0:T(8,128)}), f32[4,128,448]{1,2,0:T(8,128)S(1)}, u32[]{:S(2)}, u32[]{:S(2)}) %all-to-all-start.5) | async-done | bytes 917536 | tf_op jit(solution)/shard_map/all_to_all | solution.py:13
  115.9 0.3 copy.27
  116.3 0.1 fusion.1
  116.4 0.1 copy.28
  116.5 0.3 copy.29
  116.8 3.4 %add_divide_fusion = (f32[512,448]{0,1:T(8,128)}, f32[512,448]{0,1:T(8,128)}, f32[512,448]{0,1:T(8,128)}) fusion(f32[512,448]{0,1:T(8,128)S(1)} %copy.29, f32[512,448]{0,1:T(8,128)} %param.9, f32[512,448]{0,1:T(8,128)} %param.8), kind=kLoop, calls=%fused_computation.11 | loop fusion | flops 2523136 | bytes 5505024 | tf_op jit(solution)/shard_map/div | solution.py:56
  120.2 1.5 %copy.32 = f32[512,448]{1,0:T(8,128)S(1)} copy(f32[512,448]{0,1:T(8,128)} %get-tuple-element.3) | data formatting | bytes 1835008 | tf_op jit(solution)/shard_map/div | solution.py:56
  121.7 0.1 copy.38
  121.8 0.0 copy-start.2
  121.8 0.0 copy-start.3
  121.8 0.1 reverse_select_fusion
  121.9 0.9 copy-done.2
  122.8 0.3 copy-done.3
  123.1 2.1 %fusion = f32[512,448]{0,1:T(8,128)} fusion(f32[512,448]{1,0:T(8,128)S(1)} %bitcast.26, f32[512,448]{0,1:T(8,128)S(1)} %copy-done.3, f32[256,512]{1,0:T(8,128)S(1)} %copy-done.2, f32[256,512]{1,0:T(8,128)S(1)} %bitcast.23), kind=kOutput, calls=%fused_computation.4 | convolution fusion | flops 705593344 | bytes 3801088 | tf_op jit(solution)/shard_map/dot_general | solution.py:28
  (4 shorter events, 0.1 us)
Async XLA Ops:
  0.6 59.7 %copy-start = (f32[512,448]{0,1:T(8,128)S(1)}, f32[512,448]{0,1:T(8,128)}, u32[]{:S(2)}) copy-start(f32[512,448]{0,1:T(8,128)} %param.5) | copy-start | bytes 2752516
  56.6 3.8 %collective-permute-start = (f32[256,512]{1,0:T(8,128)S(1)}, f32[256,512]{1,0:T(8,128)S(1)}, u32[]{:S(2)}, u32[]{:S(2)}) collective-permute-start(f32[256,512]{1,0:T(8,128)S(1)} %bitcast.21), channel_id=1, source_target_pairs={{0,1},{1,0},{2,3},{3,2},{4,5},{5,4},{6,7},{7,6},{8,9},{9,8},{10,11... | collective-permute-start | bytes 1572872 | tf_op jit(solution)/shard_map/ppermute | solution.py:39
  60.4 0.9 copy-start.1
  101.6 14.3 %all-to-all-start.5 = ((f32[4,128,448]{1,2,0:T(8,128)}), f32[4,128,448]{1,2,0:T(8,128)S(1)}, u32[]{:S(2)}, u32[]{:S(2)}) async-start(f32[4,128,448]{1,2,0:T(8,128)} %broadcast_in_dim.31), calls=%async_computation.5 | async-start | bytes 1835008 | tf_op jit(solution)/shard_map/all_to_all | solution.py:13
  121.8 1.0 copy-start.2
  121.8 1.3 %copy-start.3 = (f32[512,448]{0,1:T(8,128)S(1)}, f32[512,448]{0,1:T(8,128)}, u32[]{:S(2)}) copy-start(f32[512,448]{0,1:T(8,128)} %param.6) | copy-start | bytes 2752516

commit v2 on v1

v2 whole, which is shorter than its diff:
```python
import jax
import jax.numpy as jnp
from jax import lax
from jax.experimental import pallas as pl
from jax.experimental.pallas import tpu as pltpu
from jax.sharding import Mesh, PartitionSpec as P

STEP = 100
CORR_ONE = 1.0 - 0.9**STEP
CORR_TWO = 1.0 - 0.999**STEP
SPLIT = (("x", 4), ("zl", 4), ("y", 8), ("zh", 4), ("core", 2))
ROW = ("x", "zl")
COL = ("y", "zh", "core")
VMEM = pl.BlockSpec(memory_space=pltpu.VMEM)
SMEM = pl.BlockSpec(memory_space=pltpu.SMEM)
HBM = pl.BlockSpec(memory_space=pl.ANY)
PARAMS = pltpu.CompilerParams(vmem_limit_bytes=40 * 1024 * 1024)


def split(a):
    high = a.astype(jnp.bfloat16)
    return high, (a - high.astype(jnp.float32)).astype(jnp.bfloat16)


def product(a, b, dims):
    def one(left, right):
        return lax.dot_general(
            left, right, (dims, ((), ())), preferred_element_type=jnp.float32
        )

    return one(a[0], b[1]) + one(a[1], b[0]) + one(a[0], b[0])


def project_kernel(core_ref, mine_ref, other_ref, grad_ref, low_ref, high_ref, rest_ref, order_ref):
    first = core_ref[0] == 0
    order_ref[:, 0] = jnp.where(first, mine_ref[...], other_ref[...])
    order_ref[:, 1] = jnp.where(first, other_ref[...], mine_ref[...])
    high, rest = split(order_ref[...].reshape(high_ref.shape))
    high_ref[...] = high
    rest_ref[...] = rest
    parts, lanes, rows, width = low_ref.shape
    for i in range(parts):
        grad = split(grad_ref[i * rows : (i + 1) * rows, :])
        low = product(grad, (high_ref[...], rest_ref[...]), ((1,), (1,)))
        for j in range(lanes):
            low_ref[i, j] = low[:, j * width : (j + 1) * width]


def spread_kernel(blocks_ref, out_ref):
    total = blocks_ref[0]
    for i in range(1, blocks_ref.shape[0]):
        total = total + blocks_ref[i]
    for i in range(out_ref.shape[0]):
        out_ref[i] = total


def step_kernel(
    low_ref, first_ref, second_ref, weight_ref, high_ref, rest_ref,
    new_first_hbm, new_second_hbm, update_hbm,
    new_first, new_second, update, normed_high, normed_rest, sems,
):
    parts, lanes, rows, width = low_ref.shape
    copies = []
    for i in range(parts):
        here = slice(i * rows, (i + 1) * rows)
        for j in range(lanes):
            at = (here, slice(j * width, (j + 1) * width))
            low = low_ref[i, j]
            one = 0.9 * first_ref[at] + 0.1 * low
            two = 0.999 * second_ref[at] + 0.001 * low * low
            new_first[at] = one
            new_second[at] = two
            normed = (one / CORR_ONE) / (jnp.sqrt(two / CORR_TWO) + 1e-08)
            normed_high[at], normed_rest[at] = split(normed)
        total = product(
            (normed_high[here, :], normed_rest[here, :]),
            (high_ref[...], rest_ref[...]),
            ((1,), (0,)),
        )
        update[here, :] = 0.25 * total + 0.1 * weight_ref[here, :]
        pairs = ((new_first, new_first_hbm), (new_second, new_second_hbm), (update, update_hbm))
        for k, (source, target) in enumerate(pairs):
            copy = pltpu.make_async_copy(source.at[here, :], target.at[here, :], sems.at[i, k])
            copy.start()
            copies.append(copy)
    for copy in copies:
        copy.wait()


def project(core, mine, other, grad, parts, lanes):
    ff, depth = grad.shape
    rank = mine.shape[0] * mine.shape[1] * 2
    return pl.pallas_call(
        project_kernel,
        out_shape=(
            jax.ShapeDtypeStruct((parts, lanes, ff // parts, rank // lanes), jnp.float32),
            jax.ShapeDtypeStruct((rank, depth), jnp.bfloat16),
            jax.ShapeDtypeStruct((rank, depth), jnp.bfloat16),
        ),
        in_specs=[SMEM, VMEM, VMEM, VMEM],
        out_specs=(VMEM,) * 3,
        scratch_shapes=[pltpu.VMEM((mine.shape[0], 2) + mine.shape[1:], jnp.float32)],
        compiler_params=PARAMS,
        name="project",
    )(core, mine, other, grad)


def spread(blocks, copies):
    return pl.pallas_call(
        spread_kernel,
        out_shape=jax.ShapeDtypeStruct((copies,) + blocks.shape[1:], jnp.float32),
        in_specs=[VMEM],
        out_specs=VMEM,
        compiler_params=PARAMS,
        name="spread",
    )(blocks)


def step(low, first, second, weight, high, rest):
    shape = jax.ShapeDtypeStruct(first.shape, jnp.float32)
    wide = pltpu.VMEM(first.shape, jnp.float32)
    wide_out = pltpu.VMEM(weight.shape, jnp.float32)
    half = pltpu.VMEM(first.shape, jnp.bfloat16)
    return pl.pallas_call(
        step_kernel,
        out_shape=(shape, shape, jax.ShapeDtypeStruct(weight.shape, jnp.float32)),
        in_specs=[VMEM] * 6,
        out_specs=(HBM,) * 3,
        scratch_shapes=[wide, wide, wide_out, half, half, pltpu.SemaphoreType.DMA((low.shape[0], 3))],
        compiler_params=PARAMS,
        name="step",
    )(low, first, second, weight, high, rest)


def exchange(blocks, axis):
    return lax.all_to_all(blocks, axis, 0, 0)


def gather(block, axis):
    return exchange(jnp.broadcast_to(block[None], (lax.axis_size(axis),) + block.shape), axis)


def body(gradient, weight, projector, first_moment, second_moment):
    share = projector.shape[1]
    depth = projector.shape[0]
    xs, zs = lax.axis_size("x"), lax.axis_size("zl")
    mine = gather(gather(projector.T, "zh"), "y").reshape(-1, share, depth)
    other = lax.ppermute(mine, "core", [(0, 1), (1, 0)])
    core = lax.axis_index("core").astype(jnp.int32).reshape(1)
    low, high, rest = project(core, mine, other, gradient.T, xs, zs)
    low = jnp.sum(exchange(low, "x"), 0)
    low = spread(exchange(low, "zl"), xs * zs)
    low = exchange(low, ROW)
    low = low.reshape((xs, zs) + low.shape[1:])
    outs = step(low, first_moment.T, second_moment.T, weight.T, high, rest)
    return tuple(out.T for out in outs)


def solution(mesh):
    sizes = tuple(size for _, size in SPLIT)
    axes = tuple(name for name, _ in SPLIT)
    fine = Mesh(mesh.devices.reshape(sizes), axes)
    return jax.shard_map(
        body,
        mesh=fine,
        in_specs=(P(ROW, COL), P(ROW, COL), P(ROW, COL), P(None, COL), P(None, COL)),
        out_specs=(P(None, COL), P(None, COL), P(ROW, COL)),
        check_vma=False,
    )
```

time: 126 us -> 120 us (0.952)
  the two profiles are of different devices: /device:TPU:2 before, /device:TPU:1 now
where the time goes in v2:
time: 120 us
  blocking collectives  106 us (88%)
  starting transfers between devices  6.1 us (5%)
  Pallas kernels  4.61 us (4%)
  waiting for transfers between devices  1.51 us (1%)
    all_to_all x5, blocking collectives, exchange(): return lax.all_to_all(blocks, axis, 0, 0)  106 us
    ppermute x1, starting transfers between devices, body(): other = lax.ppermute(mine, 'core', [(0, 1), (1, 0)])  6.1 us
    pallas_call x1, Pallas kernels, step(): pl.pallas_call(step_kernel, out_shape=(shape, shape, jax.ShapeDtypeStruct...  2.44 us
  transfers between devices with their start and end apart: 1, of which 1 were waited for; matrix products, arithmetic and copies ran while one was open for 0% of the time, Pallas kernels for 0%

profile of v2, /device:TPU:1, one launch (start us, length us, event | category | flops | bytes accessed | tf_op | source)
XLA Modules:
  0.0 119.8 jit_solution(17226115460634184951)
XLA Ops:
  0.6 0.0 copy-start.3
  0.6 0.8 broadcast_in_dim.4
  1.4 31.5 %all_to_all.25 = f32[4,8,512]{2,1,0:T(8,128)S(1)} all-to-all(f32[4,8,512]{2,1,0:T(8,128)S(1)} %broadcast_in_dim.4), channel_id=1, replica_groups=mesh['x'=4,'zl'=4,'y'=8,'zh'=4,'core'=2] {'zh'}, dimensions={0} | all-to-all | bytes 131072 | tf_op jit(solution)/shard_map/all_to_all | solution.py:136
  33.0 20.9 %all_to_all.26 = f32[8,4,8,512]{3,2,1,0:T(8,128)S(1)} all-to-all(f32[8,4,8,512]{3,2,1,0:T(8,128)S(1)} %broadcast_in_dim.5), channel_id=1, replica_groups=mesh['x'=4,'zl'=4,'y'=8,'zh'=4,'core'=2] {'y'}, dimensions={0} | all-to-all | bytes 1048576 | tf_op jit(solution)/shard_map/all_to_all | solution.py:136
  53.9 6.1 %collective-permute-start = (f32[32,8,512]{2,1,0:T(8,128)S(1)}, f32[32,8,512]{2,1,0:T(8,128)S(1)}, u32[]{:S(2)}, u32[]{:S(2)}) collective-permute-start(f32[32,8,512]{2,1,0:T(8,128)S(1)} %bitcast.12), channel_id=1, source_target_pairs={{0,1},{1,0},{2,3},{3,2},{4,5},{5,4},{6,7},{7,6},{8,9},{9,8},{10,11... | collective-permute-start | bytes 1572872 | tf_op jit(solution)/shard_map/ppermute | solution.py:148
  60.0 1.5 %collective-permute-done.other_ref = f32[32,8,512]{2,1,0:T(8,128)S(1)} collective-permute-done((f32[32,8,512]{2,1,0:T(8,128)S(1)}, f32[32,8,512]{2,1,0:T(8,128)S(1)}, u32[]{:S(2)}, u32[]{:S(2)}) %collective-permute-start) | collective-permute-done | bytes 524320 | tf_op jit(solution)/shard_map/ppermute | solution.py:148
  61.5 0.0 copy-done.3
  61.5 2.1 %project.1 = (f32[4,4,112,128]{3,2,1,0:T(8,128)S(1)}, bf16[512,512]{1,0:T(8,128)(2,1)S(1)}, bf16[512,512]{1,0:T(8,128)(2,1)S(1)}) custom-call(s32[1]{0:T(128)} %bitcast.core_ref, f32[32,8,512]{2,1,0:T(8,128)S(1)} %bitcast.13, f32[32,8,512]{2,1,0:T(8,128)S(1)} %collective-permute-done.other_ref, f32[448,512]{1,0:T(8,128)S(1)} %bitcast.17), custom_call_target="tpu_custom_call" | custom-call | tf_op jit(solution)/shard_map/project/pallas_call | solution.py:93
  63.6 16.6 %all_to_all.27 = f32[4,4,112,128]{3,2,1,0:T(8,128)S(1)} all-to-all(f32[4,4,112,128]{3,2,1,0:T(8,128)S(1)} %get-tuple-element.9), channel_id=1, replica_groups=mesh['x'=4,'zl'=4,'y'=8,'zh'=4,'core'=2] {'x'}, dimensions={0} | all-to-all | bytes 1835008 | tf_op jit(solution)/shard_map/all_to_all | solution.py:136
  80.2 0.1 reduce_sum.9
  80.3 9.2 %all_to_all.28.blocks_ref = f32[4,112,128]{2,1,0:T(8,128)S(1)} all-to-all(f32[4,112,128]{2,1,0:T(8,128)S(1)} %reduce_sum.9), channel_id=1, replica_groups=mesh['x'=4,'zl'=4,'y'=8,'zh'=4,'core'=2] {'zl'}, dimensions={0} | all-to-all | bytes 458752 | tf_op jit(solution)/shard_map/all_to_all | solution.py:136
  89.5 0.0 copy-start.2
  89.5 0.1 spread.1
  89.6 0.0 copy-start
  89.6 0.0 copy-start.1
  89.6 27.7 %all_to_all.29 = f32[16,112,128]{2,1,0:T(8,128)S(1)} all-to-all(f32[16,112,128]{2,1,0:T(8,128)S(1)} %spread.1), channel_id=1, replica_groups=mesh['x'=4,'zl'=4,'y'=8,'zh'=4,'core'=2] {'x','zl'}, dimensions={0} | all-to-all | bytes 1835008 | tf_op jit(solution)/shard_map/all_to_all | solution.py:136
  117.3 0.0 copy-done.2
  117.3 0.0 copy-done
  117.3 0.0 copy-done.1
  117.3 2.4 %step.1 = (f32[448,512]{1,0:T(8,128)}, f32[448,512]{1,0:T(8,128)}, f32[448,512]{1,0:T(8,128)}) custom-call(f32[4,4,112,128]{3,2,1,0:T(8,128)S(1)} %bitcast.11, f32[448,512]{1,0:T(8,128)S(1)} %bitcast.14, f32[448,512]{1,0:T(8,128)S(1)} %bitcast.15, f32[448,512]{1,0:T(8,128)S(1)} %bitcast.16, bf16[512,512]{1,0:T(8,128)(2,1)S(1)} %get-tuple-element.10.high_ref, ...), custom_call_target="tpu_custom_call" | custom-call | tf_op jit(solution)/shard_map/step/pallas_call | solution.py:124
  (1 shorter events, 0.0 us)
Async XLA Ops:
  0.6 60.9 %copy-start.3 = (f32[512,448]{0,1:T(8,128)S(1)}, f32[512,448]{0,1:T(8,128)}, u32[]{:S(2)}) copy-start(f32[512,448]{0,1:T(8,128)} %param.5) | copy-start | bytes 2752516
  53.9 7.6 %collective-permute-start = (f32[32,8,512]{2,1,0:T(8,128)S(1)}, f32[32,8,512]{2,1,0:T(8,128)S(1)}, u32[]{:S(2)}, u32[]{:S(2)}) collective-permute-start(f32[32,8,512]{2,1,0:T(8,128)S(1)} %bitcast.12), channel_id=1, source_target_pairs={{0,1},{1,0},{2,3},{3,2},{4,5},{5,4},{6,7},{7,6},{8,9},{9,8},{10,11... | collective-permute-start | bytes 1572872 | tf_op jit(solution)/shard_map/ppermute | solution.py:148
  89.5 27.8 %copy-start.2 = (f32[512,448]{0,1:T(8,128)S(1)}, f32[512,448]{0,1:T(8,128)}, u32[]{:S(2)}) copy-start(f32[512,448]{0,1:T(8,128)} %param.6) | copy-start | bytes 2752516
  89.6 27.7 %copy-start = (f32[512,448]{0,1:T(8,128)S(1)}, f32[512,448]{0,1:T(8,128)}, u32[]{:S(2)}) copy-start(f32[512,448]{0,1:T(8,128)} %param.8) | copy-start | bytes 2752516
  89.6 27.7 %copy-start.1 = (f32[512,448]{0,1:T(8,128)S(1)}, f32[512,448]{0,1:T(8,128)}, u32[]{:S(2)}) copy-start(f32[512,448]{0,1:T(8,128)} %param.9) | copy-start | bytes 2752516

commit v3 on v2

v3 whole, which is shorter than its diff:
```python
import jax
import jax.numpy as jnp
from jax import lax
from jax.experimental import pallas as pl
from jax.experimental.pallas import tpu as pltpu
from jax.sharding import Mesh, PartitionSpec as P

STEP = 100
CORR_ONE = 1.0 - 0.9**STEP
CORR_TWO = 1.0 - 0.999**STEP
SPLIT = (("x", 4), ("zl", 4), ("y", 8), ("zh", 4), ("core", 2))
ROW = ("x", "zl")
COL = ("y", "zh", "core")
VMEM = pl.BlockSpec(memory_space=pltpu.VMEM)
SMEM = pl.BlockSpec(memory_space=pltpu.SMEM)
HBM = pl.BlockSpec(memory_space=pl.ANY)
PARAMS = pltpu.CompilerParams(vmem_limit_bytes=12 * 1024 * 1024)


def split(a):
    high = a.astype(jnp.bfloat16)
    return high, (a - high.astype(jnp.float32)).astype(jnp.bfloat16)


def product(a, b, dims):
    def one(left, right):
        return lax.dot_general(
            left, right, (dims, ((), ())), preferred_element_type=jnp.float32
        )

    return one(a[0], b[1]) + one(a[1], b[0]) + one(a[0], b[0])


def halve_kernel(grad_ref, after_ref, high_ref, rest_ref):
    high_ref[...], rest_ref[...] = split(grad_ref[...])


def project_kernel(
    core_ref, mine_ref, other_ref, grad_high_ref, grad_rest_ref,
    low_ref, high_ref, rest_hbm, order_ref, rest_ref, sem,
):
    first = core_ref[0] == 0
    order_ref[:, 0] = jnp.where(first, mine_ref[...], other_ref[...])
    order_ref[:, 1] = jnp.where(first, other_ref[...], mine_ref[...])
    high, rest = split(order_ref[...].reshape(high_ref.shape))
    high_ref[...] = high
    rest_ref[...] = rest
    keep = pltpu.make_async_copy(rest_ref, rest_hbm, sem)
    keep.start()
    parts, rows, _ = low_ref.shape
    for i in range(parts):
        here = slice(i * rows, (i + 1) * rows)
        grad = grad_high_ref[here, :], grad_rest_ref[here, :]
        low_ref[i] = product(grad, (high_ref[...], rest_ref[...]), ((1,), (1,)))
    keep.wait()


def step_kernel(
    low_ref, first_ref, second_ref, weight_ref, high_ref, rest_ref,
    new_first_hbm, new_second_hbm, update_hbm,
    new_first, new_second, update, normed_high, normed_rest, sems,
):
    parts, rows, _ = low_ref.shape
    copies = []
    for i in range(parts):
        here = slice(i * rows, (i + 1) * rows)
        low = low_ref[i]
        one = 0.9 * first_ref[here, :] + 0.1 * low
        two = 0.999 * second_ref[here, :] + 0.001 * low * low
        new_first[here, :] = one
        new_second[here, :] = two
        normed = (one / CORR_ONE) / (jnp.sqrt(two / CORR_TWO) + 1e-08)
        normed_high[here, :], normed_rest[here, :] = split(normed)
        total = product(
            (normed_high[here, :], normed_rest[here, :]),
            (high_ref[...], rest_ref[...]),
            ((1,), (0,)),
        )
        update[here, :] = 0.25 * total + 0.1 * weight_ref[here, :]
        pairs = ((new_first, new_first_hbm), (new_second, new_second_hbm), (update, update_hbm))
        for k, (source, target) in enumerate(pairs):
            copy = pltpu.make_async_copy(source.at[here, :], target.at[here, :], sems.at[i, k])
            copy.start()
            copies.append(copy)
    for copy in copies:
        copy.wait()


def halve(grad, after):
    part = jax.ShapeDtypeStruct(grad.shape, jnp.bfloat16)
    return pl.pallas_call(
        halve_kernel,
        out_shape=(part, part),
        in_specs=[VMEM, HBM],
        out_specs=(VMEM,) * 2,
        compiler_params=PARAMS,
        name="halve",
    )(grad, after)


def project(core, mine, other, grad, parts):
    ff, depth = grad[0].shape
    rank = mine.shape[0] * mine.shape[1] * 2
    half = jax.ShapeDtypeStruct((rank, depth), jnp.bfloat16)
    return pl.pallas_call(
        project_kernel,
        out_shape=(jax.ShapeDtypeStruct((parts, ff // parts, rank), jnp.float32), half, half),
        in_specs=[SMEM] + [VMEM] * 4,
        out_specs=(VMEM, VMEM, HBM),
        scratch_shapes=[
            pltpu.VMEM((mine.shape[0], 2) + mine.shape[1:], jnp.float32),
            pltpu.VMEM((rank, depth), jnp.bfloat16),
            pltpu.SemaphoreType.DMA,
        ],
        compiler_params=PARAMS,
        name="project",
    )(core, mine, other, *grad)


def step(low, first, second, weight, high, rest):
    shape = jax.ShapeDtypeStruct(first.shape, jnp.float32)
    wide = pltpu.VMEM(first.shape, jnp.float32)
    wide_out = pltpu.VMEM(weight.shape, jnp.float32)
    half = pltpu.VMEM(first.shape, jnp.bfloat16)
    return pl.pallas_call(
        step_kernel,
        out_shape=(shape, shape, jax.ShapeDtypeStruct(weight.shape, jnp.float32)),
        in_specs=[VMEM] * 6,
        out_specs=(HBM,) * 3,
        scratch_shapes=[wide, wide, wide_out, half, half, pltpu.SemaphoreType.DMA((low.shape[0], 3))],
        compiler_params=PARAMS,
        name="step",
    )(low, first, second, weight, high, rest)


def exchange(blocks, axis):
    return lax.all_to_all(blocks, axis, 0, 0)


def gather(block, axis):
    return exchange(jnp.broadcast_to(block[None], (lax.axis_size(axis),) + block.shape), axis)


def body(gradient, weight, projector, first_moment, second_moment):
    share = projector.shape[1]
    depth = projector.shape[0]
    mine = gather(gather(projector.T, "zh"), "y").reshape(-1, share, depth)
    other = lax.ppermute(mine, "core", [(0, 1), (1, 0)])
    core = lax.axis_index("core").astype(jnp.int32).reshape(1)
    grad = halve(gradient.T, mine)
    low, high, rest = project(core, mine, other, grad, lax.axis_size("x"))
    low = jnp.sum(exchange(low, "x"), 0)
    low = jnp.sum(lax.all_gather(low, "zl"), 0)
    low = gather(low, "x")
    outs = step(low, first_moment.T, second_moment.T, weight.T, high, rest)
    return tuple(out.T for out in outs)


def solution(mesh):
    sizes = tuple(size for _, size in SPLIT)
    axes = tuple(name for name, _ in SPLIT)
    fine = Mesh(mesh.devices.reshape(sizes), axes)
    return jax.shard_map(
        body,
        mesh=fine,
        in_specs=(P(ROW, COL), P(ROW, COL), P(ROW, COL), P(None, COL), P(None, COL)),
        out_specs=(P(None, COL), P(None, COL), P(ROW, COL)),
        check_vma=False,
    )
```

time: 120 us -> 116 us (0.967)
  the two profiles are of different devices: /device:TPU:1 before, /device:TPU:2 now
where the time goes in v3:
time: 116 us; the launch traced here: 115 us
  blocking collectives  105 us (91%)
  Pallas kernels  4.7 us (4%)
  starting transfers between devices  1.91 us (2%)
  waiting for transfers between devices  1.73 us (1%)
    all_to_all x4, blocking collectives, exchange(): return lax.all_to_all(blocks, axis, 0, 0)  85 us
    all_gather x1, blocking collectives, body(): low = jnp.sum(lax.all_gather(low, 'zl'), 0)  20.3 us
  transfers between devices with their start and end apart: 1, of which 1 were waited for; matrix products, arithmetic and copies ran while one was open for 0% of the time, Pallas kernels for 0%

profile of v3, /device:TPU:2, one launch (start us, length us, event | category | flops | bytes accessed | tf_op | source)
XLA Modules:
  0.0 115.5 jit_solution(7456560641939759108)
XLA Ops:
  0.6 0.0 copy-start.3
  0.6 0.8 broadcast_in_dim.6
  1.4 32.5 %all_to_all.20 = f32[4,8,512]{2,1,0:T(8,128)S(1)} all-to-all(f32[4,8,512]{2,1,0:T(8,128)S(1)} %broadcast_in_dim.6), channel_id=1, replica_groups=mesh['x'=4,'zl'=4,'y'=8,'zh'=4,'core'=2] {'zh'}, dimensions={0} | all-to-all | bytes 131072 | tf_op jit(solution)/shard_map/all_to_all | solution.py:137
  34.0 22.5 %all_to_all.21 = f32[8,4,8,512]{3,2,1,0:T(8,128)S(1)} all-to-all(f32[8,4,8,512]{3,2,1,0:T(8,128)S(1)} %broadcast_in_dim.7), channel_id=1, replica_groups=mesh['x'=4,'zl'=4,'y'=8,'zh'=4,'core'=2] {'y'}, dimensions={0} | all-to-all | bytes 1048576 | tf_op jit(solution)/shard_map/all_to_all | solution.py:137
  56.6 1.9 %collective-permute-start = (f32[32,8,512]{2,1,0:T(8,128)S(1)}, f32[32,8,512]{2,1,0:T(8,128)S(1)}, u32[]{:S(2)}, u32[]{:S(2)}) collective-permute-start(f32[32,8,512]{2,1,0:T(8,128)S(1)} %bitcast.11), channel_id=1, source_target_pairs={{0,1},{1,0},{2,3},{3,2},{4,5},{5,4},{6,7},{7,6},{8,9},{9,8},{10,11... | collective-permute-start | bytes 1572872 | tf_op jit(solution)/shard_map/ppermute | solution.py:148
  58.5 0.0 copy-done.3
  58.5 0.1 halve.1
  58.6 1.7 %collective-permute-done.other_ref = f32[32,8,512]{2,1,0:T(8,128)S(1)} collective-permute-done((f32[32,8,512]{2,1,0:T(8,128)S(1)}, f32[32,8,512]{2,1,0:T(8,128)S(1)}, u32[]{:S(2)}, u32[]{:S(2)}) %collective-permute-start) | collective-permute-done | bytes 524320 | tf_op jit(solution)/shard_map/ppermute | solution.py:148
  60.4 2.3 %project.1 = (f32[4,112,512]{2,1,0:T(8,128)S(1)}, bf16[512,512]{1,0:T(8,128)(2,1)S(1)}, bf16[512,512]{1,0:T(8,128)(2,1)S(1)}) custom-call(s32[1]{0:T(128)} %bitcast.core_ref, f32[32,8,512]{2,1,0:T(8,128)S(1)} %bitcast.13, f32[32,8,512]{2,1,0:T(8,128)S(1)} %collective-permute-done.other_ref, bf16[448,512]{1,0:T(8,128)(2,1)S(1)} %get-tuple-element.11.grad_high_ref, ...), custom_call_target="tpu_custom_call" | custom-call | tf_op jit(solution)/shard_map/project/pallas_call | solution.py:105
  62.7 17.2 %all_to_all.22 = f32[4,112,512]{2,1,0:T(8,128)S(1)} all-to-all(f32[4,112,512]{2,1,0:T(8,128)S(1)} %get-tuple-element.13), channel_id=1, replica_groups=mesh['x'=4,'zl'=4,'y'=8,'zh'=4,'core'=2] {'x'}, dimensions={0} | all-to-all | bytes 1835008 | tf_op jit(solution)/shard_map/all_to_all | solution.py:137
  79.8 0.1 reduce_sum.18
  79.9 20.3 %all-gather = f32[448,512]{1,0:T(8,128)S(1)} all-gather(f32[112,512]{1,0:T(8,128)S(1)} %reduce_sum.18), channel_id=2, replica_groups=mesh['x'=4,'zl'=4,'y'=8,'zh'=4,'core'=2] {'zl'}, dimensions={0}, use_global_device_ids=true | all-gather | bytes 1146880 | tf_op jit(solution)/shard_map/all_gather | solution.py:153
  100.2 0.1 reduce_sum.19
  100.3 0.0 copy-start.2
  100.3 0.1 broadcast_in_dim.8
  100.4 0.0 copy-start
  100.4 0.0 copy-start.1
  100.4 12.7 %all_to_all.23.low_ref = f32[4,112,512]{2,1,0:T(8,128)S(1)} all-to-all(f32[4,112,512]{2,1,0:T(8,128)S(1)} %broadcast_in_dim.8), channel_id=1, replica_groups=mesh['x'=4,'zl'=4,'y'=8,'zh'=4,'core'=2] {'x'}, dimensions={0} | all-to-all | bytes 1835008 | tf_op jit(solution)/shard_map/all_to_all | solution.py:137
  113.2 0.0 copy-done.2
  113.2 0.0 copy-done
  113.2 0.0 copy-done.1
  113.2 2.3 %step.1 = (f32[448,512]{1,0:T(8,128)}, f32[448,512]{1,0:T(8,128)}, f32[448,512]{1,0:T(8,128)}) custom-call(f32[4,112,512]{2,1,0:T(8,128)S(1)} %all_to_all.23.low_ref, f32[448,512]{1,0:T(8,128)S(1)} %bitcast.14, f32[448,512]{1,0:T(8,128)S(1)} %bitcast.15, f32[448,512]{1,0:T(8,128)S(1)} %bitcast.16, bf16[512,512]{1,0:T(8,128)(2,1)S(1)} %get-tuple-element.14.high_ref, ...), custom_call_target="tpu_custom_call" | custom-call | tf_op jit(solution)/shard_map/step/pallas_call | solution.py:125
  (1 shorter events, 0.0 us)
Async XLA Ops:
  0.6 57.9 %copy-start.3 = (f32[512,448]{0,1:T(8,128)S(1)}, f32[512,448]{0,1:T(8,128)}, u32[]{:S(2)}) copy-start(f32[512,448]{0,1:T(8,128)} %param.5) | copy-start | bytes 2752516
  56.6 3.8 %collective-permute-start = (f32[32,8,512]{2,1,0:T(8,128)S(1)}, f32[32,8,512]{2,1,0:T(8,128)S(1)}, u32[]{:S(2)}, u32[]{:S(2)}) collective-permute-start(f32[32,8,512]{2,1,0:T(8,128)S(1)} %bitcast.11), channel_id=1, source_target_pairs={{0,1},{1,0},{2,3},{3,2},{4,5},{5,4},{6,7},{7,6},{8,9},{9,8},{10,11... | collective-permute-start | bytes 1572872 | tf_op jit(solution)/shard_map/ppermute | solution.py:148
  100.3 12.9 %copy-start.2 = (f32[512,448]{0,1:T(8,128)S(1)}, f32[512,448]{0,1:T(8,128)}, u32[]{:S(2)}) copy-start(f32[512,448]{0,1:T(8,128)} %param.6) | copy-start | bytes 2752516
  100.4 12.8 %copy-start = (f32[512,448]{0,1:T(8,128)S(1)}, f32[512,448]{0,1:T(8,128)}, u32[]{:S(2)}) copy-start(f32[512,448]{0,1:T(8,128)} %param.8) | copy-start | bytes 2752516
  100.4 12.8 %copy-start.1 = (f32[512,448]{0,1:T(8,128)S(1)}, f32[512,448]{0,1:T(8,128)}, u32[]{:S(2)}) copy-start(f32[512,448]{0,1:T(8,128)} %param.9) | copy-start | bytes 2752516

commit v4 on v3

--- a/solution.py
+++ b/solution.py
@@ -8,8 +8,9 @@
 STEP = 100
 CORR_ONE = 1.0 - 0.9**STEP
 CORR_TWO = 1.0 - 0.999**STEP
-SPLIT = (("x", 4), ("zl", 4), ("y", 8), ("zh", 4), ("core", 2))
-ROW = ("x", "zl")
+SPLIT = (("x", 4), ("pair", 2), ("near", 2), ("y", 8), ("zh", 4), ("core", 2))
+ROW = ("x", "pair", "near")
+NEAR = ("x", "near")
 COL = ("y", "zh", "core")
 VMEM = pl.BlockSpec(memory_space=pltpu.VMEM)
 SMEM = pl.BlockSpec(memory_space=pltpu.SMEM)
@@ -47,41 +48,33 @@
     rest_ref[...] = rest
     keep = pltpu.make_async_copy(rest_ref, rest_hbm, sem)
     keep.start()
-    parts, rows, _ = low_ref.shape
-    for i in range(parts):
-        here = slice(i * rows, (i + 1) * rows)
-        grad = grad_high_ref[here, :], grad_rest_ref[here, :]
-        low_ref[i] = product(grad, (high_ref[...], rest_ref[...]), ((1,), (1,)))
+    grad = grad_high_ref[...], grad_rest_ref[...]
+    low = product(grad, (high_ref[...], rest_ref[...]), ((1,), (1,)))
+    low_ref[...] = low.reshape(low_ref.shape)
     keep.wait()
 
 
 def step_kernel(
     low_ref, first_ref, second_ref, weight_ref, high_ref, rest_ref,
     new_first_hbm, new_second_hbm, update_hbm,
-    new_first, new_second, update, normed_high, normed_rest, sems,
+    new_first, new_second, update, sems,
 ):
-    parts, rows, _ = low_ref.shape
-    copies = []
-    for i in range(parts):
-        here = slice(i * rows, (i + 1) * rows)
-        low = low_ref[i]
-        one = 0.9 * first_ref[here, :] + 0.1 * low
-        two = 0.999 * second_ref[here, :] + 0.001 * low * low
-        new_first[here, :] = one
-        new_second[here, :] = two
-        normed = (one / CORR_ONE) / (jnp.sqrt(two / CORR_TWO) + 1e-08)
-        normed_high[here, :], normed_rest[here, :] = split(normed)
-        total = product(
-            (normed_high[here, :], normed_rest[here, :]),
-            (high_ref[...], rest_ref[...]),
-            ((1,), (0,)),
-        )
-        update[here, :] = 0.25 * total + 0.1 * weight_ref[here, :]
-        pairs = ((new_first, new_first_hbm), (new_second, new_second_hbm), (update, update_hbm))
-        for k, (source, target) in enumerate(pairs):
-            copy = pltpu.make_async_copy(source.at[here, :], target.at[here, :], sems.at[i, k])
-            copy.start()
-            copies.append(copy)
+    def send(source, target, k):
+        copy = pltpu.make_async_copy(source, target, sems.at[k])
+        copy.start()
+        return copy
+
+    low = low_ref[...].reshape(first_ref.shape)
+    new_first[...] = 0.9 * first_ref[...] + 0.1 * low
+    copies = [send(new_first, new_first_hbm, 0)]
+    new_second[...] = 0.999 * second_ref[...] + 0.001 * low * low
+    copies.append(send(new_second, new_second_hbm, 1))
+    normed = (new_first[...] * (1.0 / CORR_ONE)) / (
+        jnp.sqrt(new_second[...] * (1.0 / CORR_TWO)) + 1e-08
+    )
+    total = product(split(normed), (high_ref[...], rest_ref[...]), ((1,), (0,)))
+    update[...] = 0.25 * total + 0.1 * weight_ref[...]
+    copies.append(send(update, update_hbm, 2))
     for copy in copies:
         copy.wait()
 
@@ -121,13 +114,12 @@
     shape = jax.ShapeDtypeStruct(first.shape, jnp.float32)
     wide = pltpu.VMEM(first.shape, jnp.float32)
     wide_out = pltpu.VMEM(weight.shape, jnp.float32)
-    half = pltpu.VMEM(first.shape, jnp.bfloat16)
     return pl.pallas_call(
         step_kernel,
         out_shape=(shape, shape, jax.ShapeDtypeStruct(weight.shape, jnp.float32)),
         in_specs=[VMEM] * 6,
         out_specs=(HBM,) * 3,
-        scratch_shapes=[wide, wide, wide_out, half, half, pltpu.SemaphoreType.DMA((low.shape[0], 3))],
+        scratch_shapes=[wide, wide, wide_out, pltpu.SemaphoreType.DMA((3,))],
         compiler_params=PARAMS,
         name="step",
     )(low, first, second, weight, high, rest)
@@ -148,10 +140,11 @@
     other = lax.ppermute(mine, "core", [(0, 1), (1, 0)])
     core = lax.axis_index("core").astype(jnp.int32).reshape(1)
     grad = halve(gradient.T, mine)
-    low, high, rest = project(core, mine, other, grad, lax.axis_size("x"))
-    low = jnp.sum(exchange(low, "x"), 0)
-    low = jnp.sum(lax.all_gather(low, "zl"), 0)
-    low = gather(low, "x")
+    blocks = lax.axis_size(NEAR)
+    low, high, rest = project(core, mine, other, grad, blocks)
+    low = jnp.sum(exchange(low, NEAR), 0)
+    low = low + lax.ppermute(low, "pair", [(0, 1), (1, 0)])
+    low = gather(low, NEAR)
     outs = step(low, first_moment.T, second_moment.T, weight.T, high, rest)
     return tuple(out.T for out in outs)
 

time: 116 us -> 108 us (0.931)
  the two profiles are of different devices: /device:TPU:2 before, /device:TPU:1 now
where the time goes in v4:
time: 108 us; the launch traced here: 107 us
  blocking collectives  86.5 us (80%)
  starting transfers between devices  10.2 us (9%)
  waiting for transfers between devices  5.27 us (5%)
  Pallas kernels  3.57 us (3%)
    all_to_all x4, blocking collectives, exchange(): return lax.all_to_all(blocks, axis, 0, 0)  86.5 us
    ppermute x1, starting transfers between devices, body(): other = lax.ppermute(mine, 'core', [(0, 1), (1, 0)])  6.1 us
    ppermute x1, starting transfers between devices, body(): low = low + lax.ppermute(low, 'pair', [(0, 1), (1, 0)])  4.07 us
    ppermute x1, waiting for transfers between devices, body(): low = low + lax.ppermute(low, 'pair', [(0, 1), (1, 0)])  3.9 us
    pallas_call x1, Pallas kernels, step(): pl.pallas_call(step_kernel, out_shape=(shape, shape, jax.ShapeDtypeStruct...  2.29 us
  transfers between devices with their start and end apart: 2, of which 2 were waited for; matrix products, arithmetic and copies ran while one was open for 0% of the time, Pallas kernels for 0%

profile of v4, /device:TPU:1, one launch (start us, length us, event | category | flops | bytes accessed | tf_op | source)
XLA Modules:
  0.0 107.3 jit_solution(8546640147618638987)
XLA Ops:
  0.6 0.0 copy-start.3
  0.6 0.8 broadcast_in_dim.6
  1.4 31.5 %all_to_all.20 = f32[4,8,512]{2,1,0:T(8,128)S(1)} all-to-all(f32[4,8,512]{2,1,0:T(8,128)S(1)} %broadcast_in_dim.6), channel_id=1, replica_groups=mesh['x'=4,'pair'=2,'near'=2,'y'=8,'zh'=4,'core'=2] {'zh'}, dimensions={0} | all-to-all | bytes 131072 | tf_op jit(solution)/shard_map/all_to_all | solution.py:129
  33.0 20.9 %all_to_all.21 = f32[8,4,8,512]{3,2,1,0:T(8,128)S(1)} all-to-all(f32[8,4,8,512]{3,2,1,0:T(8,128)S(1)} %broadcast_in_dim.7), channel_id=1, replica_groups=mesh['x'=4,'pair'=2,'near'=2,'y'=8,'zh'=4,'core'=2] {'y'}, dimensions={0} | all-to-all | bytes 1048576 | tf_op jit(solution)/shard_map/all_to_all | solution.py:129
  53.9 6.1 %collective-permute-start = (f32[32,8,512]{2,1,0:T(8,128)S(1)}, f32[32,8,512]{2,1,0:T(8,128)S(1)}, u32[]{:S(2)}, u32[]{:S(2)}) collective-permute-start(f32[32,8,512]{2,1,0:T(8,128)S(1)} %bitcast.10), channel_id=1, source_target_pairs={{0,1},{1,0},{2,3},{3,2},{4,5},{5,4},{6,7},{7,6},{8,9},{9,8},{10,11... | collective-permute-start | bytes 1572872 | tf_op jit(solution)/shard_map/ppermute | solution.py:140
  60.0 0.0 copy-done.3
  60.0 0.1 halve.1
  60.1 1.4 %collective-permute-done.other_ref = f32[32,8,512]{2,1,0:T(8,128)S(1)} collective-permute-done((f32[32,8,512]{2,1,0:T(8,128)S(1)}, f32[32,8,512]{2,1,0:T(8,128)S(1)}, u32[]{:S(2)}, u32[]{:S(2)}) %collective-permute-start) | collective-permute-done | bytes 524320 | tf_op jit(solution)/shard_map/ppermute | solution.py:140
  61.5 1.2 %project.1 = (f32[8,56,512]{2,1,0:T(8,128)S(1)}, bf16[512,512]{1,0:T(8,128)(2,1)S(1)}, bf16[512,512]{1,0:T(8,128)(2,1)S(1)}) custom-call(s32[1]{0:T(128)} %bitcast.core_ref, f32[32,8,512]{2,1,0:T(8,128)S(1)} %bitcast.12, f32[32,8,512]{2,1,0:T(8,128)S(1)} %collective-permute-done.other_ref, bf16[448,512]{1,0:T(8,128)(2,1)S(1)} %get-tuple-element.11.grad_high_ref, ...), custom_call_target="tpu_custom_call" | custom-call | tf_op jit(solution)/shard_map/project/pallas_call | solution.py:98
  62.6 17.4 %all_to_all.22 = f32[8,56,512]{2,1,0:T(8,128)S(1)} all-to-all(f32[8,56,512]{2,1,0:T(8,128)S(1)} %get-tuple-element.13), channel_id=1, replica_groups=mesh['x'=4,'pair'=2,'near'=2,'y'=8,'zh'=4,'core'=2] {'x','near'}, dimensions={0} | all-to-all | bytes 1835008 | tf_op jit(solution)/shard_map/all_to_all | solution.py:129
  80.1 0.1 reduce_sum.9
  80.2 4.1 %collective-permute-start.1 = (f32[56,512]{1,0:T(8,128)S(1)}, f32[56,512]{1,0:T(8,128)S(1)}, u32[]{:S(2)}, u32[]{:S(2)}) collective-permute-start(f32[56,512]{1,0:T(8,128)S(1)} %reduce_sum.9), channel_id=1, source_target_pairs={{0,128},{128,0},{1,129},{129,1},{2,130},{130,2},{3,131},{131,3},{4... | collective-permute-start | bytes 344072 | tf_op jit(solution)/shard_map/ppermute | solution.py:146
  84.2 3.9 %collective-permute-done.1 = f32[56,512]{1,0:T(8,128)S(1)} collective-permute-done((f32[56,512]{1,0:T(8,128)S(1)}, f32[56,512]{1,0:T(8,128)S(1)}, u32[]{:S(2)}, u32[]{:S(2)}) %collective-permute-start.1) | collective-permute-done | bytes 114720 | tf_op jit(solution)/shard_map/ppermute | solution.py:146
  88.2 0.0 copy-start.2
  88.2 0.1 broadcast_in_dim.8
  88.3 0.0 copy-start
  88.3 0.0 copy-start.1
  88.3 16.7 %all_to_all.23.low_ref = f32[8,56,512]{2,1,0:T(8,128)S(1)} all-to-all(f32[8,56,512]{2,1,0:T(8,128)S(1)} %broadcast_in_dim.8), channel_id=1, replica_groups=mesh['x'=4,'pair'=2,'near'=2,'y'=8,'zh'=4,'core'=2] {'x','near'}, dimensions={0} | all-to-all | bytes 1835008 | tf_op jit(solution)/shard_map/all_to_all | solution.py:129
  105.0 0.0 copy-done.2
  105.0 0.0 copy-done
  105.0 0.0 copy-done.1
  105.0 2.3 %step.1 = (f32[448,512]{1,0:T(8,128)}, f32[448,512]{1,0:T(8,128)}, f32[448,512]{1,0:T(8,128)}) custom-call(f32[8,56,512]{2,1,0:T(8,128)S(1)} %all_to_all.23.low_ref, f32[448,512]{1,0:T(8,128)S(1)} %bitcast.13, f32[448,512]{1,0:T(8,128)S(1)} %bitcast.14, f32[448,512]{1,0:T(8,128)S(1)} %bitcast.15, bf16[512,512]{1,0:T(8,128)(2,1)S(1)} %get-tuple-element.14.high_ref, ...), custom_call_target="tpu_custom_call" | custom-call | tf_op jit(solution)/shard_map/step/pallas_call | solution.py:117
  (2 shorter events, 0.1 us)
Async XLA Ops:
  0.6 59.3 %copy-start.3 = (f32[512,448]{0,1:T(8,128)S(1)}, f32[512,448]{0,1:T(8,128)}, u32[]{:S(2)}) copy-start(f32[512,448]{0,1:T(8,128)} %param.5) | copy-start | bytes 2752516
  53.9 7.6 %collective-permute-start = (f32[32,8,512]{2,1,0:T(8,128)S(1)}, f32[32,8,512]{2,1,0:T(8,128)S(1)}, u32[]{:S(2)}, u32[]{:S(2)}) collective-permute-start(f32[32,8,512]{2,1,0:T(8,128)S(1)} %bitcast.10), channel_id=1, source_target_pairs={{0,1},{1,0},{2,3},{3,2},{4,5},{5,4},{6,7},{7,6},{8,9},{9,8},{10,11... | collective-permute-start | bytes 1572872 | tf_op jit(solution)/shard_map/ppermute | solution.py:140
  80.2 8.0 %collective-permute-start.1 = (f32[56,512]{1,0:T(8,128)S(1)}, f32[56,512]{1,0:T(8,128)S(1)}, u32[]{:S(2)}, u32[]{:S(2)}) collective-permute-start(f32[56,512]{1,0:T(8,128)S(1)} %reduce_sum.9), channel_id=1, source_target_pairs={{0,128},{128,0},{1,129},{129,1},{2,130},{130,2},{3,131},{131,3},{4... | collective-permute-start | bytes 344072 | tf_op jit(solution)/shard_map/ppermute | solution.py:146
  88.2 16.8 %copy-start.2 = (f32[512,448]{0,1:T(8,128)S(1)}, f32[512,448]{0,1:T(8,128)}, u32[]{:S(2)}) copy-start(f32[512,448]{0,1:T(8,128)} %param.6) | copy-start | bytes 2752516
  88.3 16.7 %copy-start = (f32[512,448]{0,1:T(8,128)S(1)}, f32[512,448]{0,1:T(8,128)}, u32[]{:S(2)}) copy-start(f32[512,448]{0,1:T(8,128)} %param.8) | copy-start | bytes 2752516
  88.3 16.7 %copy-start.1 = (f32[512,448]{0,1:T(8,128)S(1)}, f32[512,448]{0,1:T(8,128)}, u32[]{:S(2)}) copy-start(f32[512,448]{0,1:T(8,128)} %param.9) | copy-start | bytes 2752516

commit v5 on v4

--- a/solution.py
+++ b/solution.py
@@ -69,9 +69,9 @@
     copies = [send(new_first, new_first_hbm, 0)]
     new_second[...] = 0.999 * second_ref[...] + 0.001 * low * low
     copies.append(send(new_second, new_second_hbm, 1))
-    normed = (new_first[...] * (1.0 / CORR_ONE)) / (
-        jnp.sqrt(new_second[...] * (1.0 / CORR_TWO)) + 1e-08
-    )
+    square = new_second[...] * (1.0 / CORR_TWO)
+    root = square * lax.rsqrt(square)
+    normed = (new_first[...] * (1.0 / CORR_ONE)) / (root + 1e-08)
     total = product(split(normed), (high_ref[...], rest_ref[...]), ((1,), (0,)))
     update[...] = 0.25 * total + 0.1 * weight_ref[...]
     copies.append(send(update, update_hbm, 2))
@@ -136,7 +136,7 @@
 def body(gradient, weight, projector, first_moment, second_moment):
     share = projector.shape[1]
     depth = projector.shape[0]
-    mine = gather(gather(projector.T, "zh"), "y").reshape(-1, share, depth)
+    mine = gather(lax.all_gather(projector.T, "zh"), "y").reshape(-1, share, depth)
     other = lax.ppermute(mine, "core", [(0, 1), (1, 0)])
     core = lax.axis_index("core").astype(jnp.int32).reshape(1)
     grad = halve(gradient.T, mine)

time: 108 us -> 104 us (0.963)
  blocking collectives: 86.5 us -> 82.6 us
  starting transfers between devices: 10.2 us -> 11.5 us
    all_to_all x4 -> x3, blocking collectives: 86.5 us -> 54.8 us  [exchange(): return lax.all_to_all(blocks, axis, 0, 0)]
    all_gather x0 -> x1, blocking collectives: none -> 27.8 us  [body(): lax.all_gather(projector.T, 'zh')]
    ppermute x1, starting transfers between devices: 6.1 us -> 7.35 us  [body(): other = lax.ppermute(mine, 'core', [(0, 1), (1, 0)])]
where the time goes in v5:
time: 104 us
  blocking collectives  82.6 us (79%)
  starting transfers between devices  11.5 us (11%)
  waiting for transfers between devices  5.2 us (5%)
  Pallas kernels  3.41 us (3%)
    all_to_all x3, blocking collectives, exchange(): return lax.all_to_all(blocks, axis, 0, 0)  54.8 us
    all_gather x1, blocking collectives, body(): lax.all_gather(projector.T, 'zh')  27.8 us
    ppermute x1, starting transfers between devices, body(): other = lax.ppermute(mine, 'core', [(0, 1), (1, 0)])  7.35 us
    ppermute x1, starting transfers between devices, body(): low = low + lax.ppermute(low, 'pair', [(0, 1), (1, 0)])  4.15 us
    ppermute x1, waiting for transfers between devices, body(): low = low + lax.ppermute(low, 'pair', [(0, 1), (1, 0)])  3.83 us
    pallas_call x1, Pallas kernels, step(): pl.pallas_call(step_kernel, out_shape=(shape, shape, jax.ShapeDtypeStruct...  2.14 us
  transfers between devices with their start and end apart: 2, of which 2 were waited for; matrix products, arithmetic and copies ran while one was open for 0% of the time, Pallas kernels for 0%

profile of v5, /device:TPU:1, one launch (start us, length us, event | category | flops | bytes accessed | tf_op | source)
XLA Modules:
  0.0 103.7 jit_solution(2782844718103941216)
XLA Ops:
  0.6 0.0 copy-start.3
  0.6 27.8 %all-gather = f32[32,512]{1,0:T(8,128)S(1)} all-gather(f32[8,512]{1,0:T(8,128)} %bitcast.19), channel_id=2, replica_groups=mesh['x'=4,'pair'=2,'near'=2,'y'=8,'zh'=4,'core'=2] {'zh'}, dimensions={0}, use_global_device_ids=true | all-gather | bytes 81920 | tf_op jit(solution)/shard_map/all_gather | solution.py:139
  28.4 0.1 broadcast_in_dim.4
  28.5 19.7 %all_to_all.15 = f32[8,4,8,512]{3,2,1,0:T(8,128)S(1)} all-to-all(f32[8,4,8,512]{3,2,1,0:T(8,128)S(1)} %broadcast_in_dim.4), channel_id=1, replica_groups=mesh['x'=4,'pair'=2,'near'=2,'y'=8,'zh'=4,'core'=2] {'y'}, dimensions={0} | all-to-all | bytes 1048576 | tf_op jit(solution)/shard_map/all_to_all | solution.py:129
  48.2 7.4 %collective-permute-start = (f32[32,8,512]{2,1,0:T(8,128)S(1)}, f32[32,8,512]{2,1,0:T(8,128)S(1)}, u32[]{:S(2)}, u32[]{:S(2)}) collective-permute-start(f32[32,8,512]{2,1,0:T(8,128)S(1)} %bitcast.11), channel_id=1, source_target_pairs={{0,1},{1,0},{2,3},{3,2},{4,5},{5,4},{6,7},{7,6},{8,9},{9,8},{10,11... | collective-permute-start | bytes 1572872 | tf_op jit(solution)/shard_map/ppermute | solution.py:140
  55.6 0.0 copy-done.3
  55.6 0.1 halve.1
  55.7 1.4 %collective-permute-done.other_ref = f32[32,8,512]{2,1,0:T(8,128)S(1)} collective-permute-done((f32[32,8,512]{2,1,0:T(8,128)S(1)}, f32[32,8,512]{2,1,0:T(8,128)S(1)}, u32[]{:S(2)}, u32[]{:S(2)}) %collective-permute-start) | collective-permute-done | bytes 524320 | tf_op jit(solution)/shard_map/ppermute | solution.py:140
  57.1 1.2 %project.1 = (f32[8,56,512]{2,1,0:T(8,128)S(1)}, bf16[512,512]{1,0:T(8,128)(2,1)S(1)}, bf16[512,512]{1,0:T(8,128)(2,1)S(1)}) custom-call(s32[1]{0:T(128)} %bitcast.core_ref, f32[32,8,512]{2,1,0:T(8,128)S(1)} %bitcast.13, f32[32,8,512]{2,1,0:T(8,128)S(1)} %collective-permute-done.other_ref, bf16[448,512]{1,0:T(8,128)(2,1)S(1)} %get-tuple-element.11.grad_high_ref, ...), custom_call_target="tpu_custom_call" | custom-call | tf_op jit(solution)/shard_map/project/pallas_call | solution.py:98
  58.3 18.2 %all_to_all.16 = f32[8,56,512]{2,1,0:T(8,128)S(1)} all-to-all(f32[8,56,512]{2,1,0:T(8,128)S(1)} %get-tuple-element.13), channel_id=1, replica_groups=mesh['x'=4,'pair'=2,'near'=2,'y'=8,'zh'=4,'core'=2] {'x','near'}, dimensions={0} | all-to-all | bytes 1835008 | tf_op jit(solution)/shard_map/all_to_all | solution.py:129
  76.5 0.1 reduce_sum.9
  76.6 4.1 %collective-permute-start.1 = (f32[56,512]{1,0:T(8,128)S(1)}, f32[56,512]{1,0:T(8,128)S(1)}, u32[]{:S(2)}, u32[]{:S(2)}) collective-permute-start(f32[56,512]{1,0:T(8,128)S(1)} %reduce_sum.9), channel_id=1, source_target_pairs={{0,128},{128,0},{1,129},{129,1},{2,130},{130,2},{3,131},{131,3},{4... | collective-permute-start | bytes 344072 | tf_op jit(solution)/shard_map/ppermute | solution.py:146
  80.7 3.8 %collective-permute-done.1 = f32[56,512]{1,0:T(8,128)S(1)} collective-permute-done((f32[56,512]{1,0:T(8,128)S(1)}, f32[56,512]{1,0:T(8,128)S(1)}, u32[]{:S(2)}, u32[]{:S(2)}) %collective-permute-start.1) | collective-permute-done | bytes 114720 | tf_op jit(solution)/shard_map/ppermute | solution.py:146
  84.6 0.0 copy-start.2
  84.6 0.1 broadcast_in_dim.5
  84.7 0.0 copy-start
  84.7 0.0 copy-start.1
  84.7 16.9 %all_to_all.17.low_ref = f32[8,56,512]{2,1,0:T(8,128)S(1)} all-to-all(f32[8,56,512]{2,1,0:T(8,128)S(1)} %broadcast_in_dim.5), channel_id=1, replica_groups=mesh['x'=4,'pair'=2,'near'=2,'y'=8,'zh'=4,'core'=2] {'x','near'}, dimensions={0} | all-to-all | bytes 1835008 | tf_op jit(solution)/shard_map/all_to_all | solution.py:129
  101.6 0.0 copy-done.2
  101.6 0.0 copy-done
  101.6 0.0 copy-done.1
  101.6 2.1 %step.1 = (f32[448,512]{1,0:T(8,128)}, f32[448,512]{1,0:T(8,128)}, f32[448,512]{1,0:T(8,128)}) custom-call(f32[8,56,512]{2,1,0:T(8,128)S(1)} %all_to_all.17.low_ref, f32[448,512]{1,0:T(8,128)S(1)} %bitcast.14, f32[448,512]{1,0:T(8,128)S(1)} %bitcast.15, f32[448,512]{1,0:T(8,128)S(1)} %bitcast.16, bf16[512,512]{1,0:T(8,128)(2,1)S(1)} %get-tuple-element.14.high_ref, ...), custom_call_target="tpu_custom_call" | custom-call | tf_op jit(solution)/shard_map/step/pallas_call | solution.py:117
  (1 shorter events, 0.0 us)
Async XLA Ops:
  0.6 55.0 %copy-start.3 = (f32[512,448]{0,1:T(8,128)S(1)}, f32[512,448]{0,1:T(8,128)}, u32[]{:S(2)}) copy-start(f32[512,448]{0,1:T(8,128)} %param.5) | copy-start | bytes 2752516
  48.2 8.9 %collective-permute-start = (f32[32,8,512]{2,1,0:T(8,128)S(1)}, f32[32,8,512]{2,1,0:T(8,128)S(1)}, u32[]{:S(2)}, u32[]{:S(2)}) collective-permute-start(f32[32,8,512]{2,1,0:T(8,128)S(1)} %bitcast.11), channel_id=1, source_target_pairs={{0,1},{1,0},{2,3},{3,2},{4,5},{5,4},{6,7},{7,6},{8,9},{9,8},{10,11... | collective-permute-start | bytes 1572872 | tf_op jit(solution)/shard_map/ppermute | solution.py:140
  76.6 8.0 %collective-permute-start.1 = (f32[56,512]{1,0:T(8,128)S(1)}, f32[56,512]{1,0:T(8,128)S(1)}, u32[]{:S(2)}, u32[]{:S(2)}) collective-permute-start(f32[56,512]{1,0:T(8,128)S(1)} %reduce_sum.9), channel_id=1, source_target_pairs={{0,128},{128,0},{1,129},{129,1},{2,130},{130,2},{3,131},{131,3},{4... | collective-permute-start | bytes 344072 | tf_op jit(solution)/shard_map/ppermute | solution.py:146
  84.6 17.0 %copy-start.2 = (f32[512,448]{0,1:T(8,128)S(1)}, f32[512,448]{0,1:T(8,128)}, u32[]{:S(2)}) copy-start(f32[512,448]{0,1:T(8,128)} %param.6) | copy-start | bytes 2752516
  84.7 16.9 %copy-start = (f32[512,448]{0,1:T(8,128)S(1)}, f32[512,448]{0,1:T(8,128)}, u32[]{:S(2)}) copy-start(f32[512,448]{0,1:T(8,128)} %param.8) | copy-start | bytes 2752516
  84.7 16.9 %copy-start.1 = (f32[512,448]{0,1:T(8,128)S(1)}, f32[512,448]{0,1:T(8,128)}, u32[]{:S(2)}) copy-start(f32[512,448]{0,1:T(8,128)} %param.9) | copy-start | bytes 2752516

commit v6 on v5

--- a/solution.py
+++ b/solution.py
@@ -143,7 +143,7 @@
     blocks = lax.axis_size(NEAR)
     low, high, rest = project(core, mine, other, grad, blocks)
     low = jnp.sum(exchange(low, NEAR), 0)
-    low = low + lax.ppermute(low, "pair", [(0, 1), (1, 0)])
+    low = jnp.sum(lax.all_gather(low, "pair"), 0)
     low = gather(low, NEAR)
     outs = step(low, first_moment.T, second_moment.T, weight.T, high, rest)
     return tuple(out.T for out in outs)

time: 104 us -> 103 us (level)
  blocking collectives: 82.6 us -> 89.4 us
  starting transfers between devices: 11.5 us -> 7.35 us
  waiting for transfers between devices: 5.2 us -> 1.37 us
    all_gather x0 -> x1, blocking collectives: none -> 6.76 us  [body(): low = jnp.sum(lax.all_gather(low, 'pair'), 0)]
    ppermute x1 -> x0, starting transfers between devices: 4.15 us -> none  [body(): low = low + lax.ppermute(low, 'pair', [(0, 1), (1, 0)])]
    ppermute x1 -> x0, waiting for transfers between devices: 3.83 us -> none  [body(): low = low + lax.ppermute(low, 'pair', [(0, 1), (1, 0)])]
  transfers between devices with their start and end apart: 2 -> 1, of which waited for: 2 -> 1; matrix products, arithmetic and copies ran while one was open for 0% -> 0% of each run, Pallas kernels for 0% -> 0%
where the time goes in v6:
time: 103 us
  blocking collectives  89.4 us (87%)
  starting transfers between devices  7.35 us (7%)
  Pallas kernels  3.41 us (3%)
  waiting for transfers between devices  1.37 us (1%)
    all_to_all x3, blocking collectives, exchange(): return lax.all_to_all(blocks, axis, 0, 0)  54.8 us
    all_gather x1, blocking collectives, body(): lax.all_gather(projector.T, 'zh')  27.8 us
    ppermute x1, starting transfers between devices, body(): other = lax.ppermute(mine, 'core', [(0, 1), (1, 0)])  7.35 us
    all_gather x1, blocking collectives, body(): low = jnp.sum(lax.all_gather(low, 'pair'), 0)  6.76 us
    pallas_call x1, Pallas kernels, step(): pl.pallas_call(step_kernel, out_shape=(shape, shape, jax.ShapeDtypeStruct...  2.14 us
  transfers between devices with their start and end apart: 1, of which 1 were waited for; matrix products, arithmetic and copies ran while one was open for 0% of the time, Pallas kernels for 0%

profile of v6, /device:TPU:1, one launch (start us, length us, event | category | flops | bytes accessed | tf_op | source)
XLA Modules:
  0.0 102.5 jit_solution(9888302222477740968)
XLA Ops:
  0.6 0.0 copy-start.3
  0.6 27.8 %all-gather = f32[32,512]{1,0:T(8,128)S(1)} all-gather(f32[8,512]{1,0:T(8,128)} %bitcast.21), channel_id=2, replica_groups=mesh['x'=4,'pair'=2,'near'=2,'y'=8,'zh'=4,'core'=2] {'zh'}, dimensions={0}, use_global_device_ids=true | all-gather | bytes 81920 | tf_op jit(solution)/shard_map/all_gather | solution.py:139
  28.4 0.1 broadcast_in_dim.4
  28.5 19.7 %all_to_all.15 = f32[8,4,8,512]{3,2,1,0:T(8,128)S(1)} all-to-all(f32[8,4,8,512]{3,2,1,0:T(8,128)S(1)} %broadcast_in_dim.4), channel_id=1, replica_groups=mesh['x'=4,'pair'=2,'near'=2,'y'=8,'zh'=4,'core'=2] {'y'}, dimensions={0} | all-to-all | bytes 1048576 | tf_op jit(solution)/shard_map/all_to_all | solution.py:129
  48.2 7.4 %collective-permute-start = (f32[32,8,512]{2,1,0:T(8,128)S(1)}, f32[32,8,512]{2,1,0:T(8,128)S(1)}, u32[]{:S(2)}, u32[]{:S(2)}) collective-permute-start(f32[32,8,512]{2,1,0:T(8,128)S(1)} %bitcast.12), channel_id=1, source_target_pairs={{0,1},{1,0},{2,3},{3,2},{4,5},{5,4},{6,7},{7,6},{8,9},{9,8},{10,11... | collective-permute-start | bytes 1572872 | tf_op jit(solution)/shard_map/ppermute | solution.py:140
  55.6 0.0 copy-done.3
  55.6 0.1 halve.1
  55.7 1.4 %collective-permute-done.other_ref = f32[32,8,512]{2,1,0:T(8,128)S(1)} collective-permute-done((f32[32,8,512]{2,1,0:T(8,128)S(1)}, f32[32,8,512]{2,1,0:T(8,128)S(1)}, u32[]{:S(2)}, u32[]{:S(2)}) %collective-permute-start) | collective-permute-done | bytes 524320 | tf_op jit(solution)/shard_map/ppermute | solution.py:140
  57.1 1.2 %project.1 = (f32[8,56,512]{2,1,0:T(8,128)S(1)}, bf16[512,512]{1,0:T(8,128)(2,1)S(1)}, bf16[512,512]{1,0:T(8,128)(2,1)S(1)}) custom-call(s32[1]{0:T(128)} %bitcast.core_ref, f32[32,8,512]{2,1,0:T(8,128)S(1)} %bitcast.14, f32[32,8,512]{2,1,0:T(8,128)S(1)} %collective-permute-done.other_ref, bf16[448,512]{1,0:T(8,128)(2,1)S(1)} %get-tuple-element.11.grad_high_ref, ...), custom_call_target="tpu_custom_call" | custom-call | tf_op jit(solution)/shard_map/project/pallas_call | solution.py:98
  58.3 18.2 %all_to_all.16 = f32[8,56,512]{2,1,0:T(8,128)S(1)} all-to-all(f32[8,56,512]{2,1,0:T(8,128)S(1)} %get-tuple-element.13), channel_id=1, replica_groups=mesh['x'=4,'pair'=2,'near'=2,'y'=8,'zh'=4,'core'=2] {'x','near'}, dimensions={0} | all-to-all | bytes 1835008 | tf_op jit(solution)/shard_map/all_to_all | solution.py:129
  76.5 0.1 reduce_sum.18
  76.6 6.8 %all-gather.1 = f32[112,512]{1,0:T(8,128)S(1)} all-gather(f32[56,512]{1,0:T(8,128)S(1)} %reduce_sum.18), channel_id=3, replica_groups=mesh['x'=4,'pair'=2,'near'=2,'y'=8,'zh'=4,'core'=2] {'pair'}, dimensions={0}, use_global_device_ids=true | all-gather | bytes 344064 | tf_op jit(solution)/shard_map/all_gather | solution.py:146
  83.4 0.0 copy-start.2
  83.4 0.1 broadcast_in_dim.5
  83.5 0.0 copy-start
  83.5 0.0 copy-start.1
  83.5 16.9 %all_to_all.17.low_ref = f32[8,56,512]{2,1,0:T(8,128)S(1)} all-to-all(f32[8,56,512]{2,1,0:T(8,128)S(1)} %broadcast_in_dim.5), channel_id=1, replica_groups=mesh['x'=4,'pair'=2,'near'=2,'y'=8,'zh'=4,'core'=2] {'x','near'}, dimensions={0} | all-to-all | bytes 1835008 | tf_op jit(solution)/shard_map/all_to_all | solution.py:129
  100.4 0.0 copy-done.2
  100.4 0.0 copy-done
  100.4 0.0 copy-done.1
  100.4 2.1 %step.1 = (f32[448,512]{1,0:T(8,128)}, f32[448,512]{1,0:T(8,128)}, f32[448,512]{1,0:T(8,128)}) custom-call(f32[8,56,512]{2,1,0:T(8,128)S(1)} %all_to_all.17.low_ref, f32[448,512]{1,0:T(8,128)S(1)} %bitcast.15, f32[448,512]{1,0:T(8,128)S(1)} %bitcast.16, f32[448,512]{1,0:T(8,128)S(1)} %bitcast.17, bf16[512,512]{1,0:T(8,128)(2,1)S(1)} %get-tuple-element.14.high_ref, ...), custom_call_target="tpu_custom_call" | custom-call | tf_op jit(solution)/shard_map/step/pallas_call | solution.py:117
  (1 shorter events, 0.0 us)
Async XLA Ops:
  0.6 55.0 %copy-start.3 = (f32[512,448]{0,1:T(8,128)S(1)}, f32[512,448]{0,1:T(8,128)}, u32[]{:S(2)}) copy-start(f32[512,448]{0,1:T(8,128)} %param.5) | copy-start | bytes 2752516
  48.2 8.9 %collective-permute-start = (f32[32,8,512]{2,1,0:T(8,128)S(1)}, f32[32,8,512]{2,1,0:T(8,128)S(1)}, u32[]{:S(2)}, u32[]{:S(2)}) collective-permute-start(f32[32,8,512]{2,1,0:T(8,128)S(1)} %bitcast.12), channel_id=1, source_target_pairs={{0,1},{1,0},{2,3},{3,2},{4,5},{5,4},{6,7},{7,6},{8,9},{9,8},{10,11... | collective-permute-start | bytes 1572872 | tf_op jit(solution)/shard_map/ppermute | solution.py:140
  83.4 17.0 %copy-start.2 = (f32[512,448]{0,1:T(8,128)S(1)}, f32[512,448]{0,1:T(8,128)}, u32[]{:S(2)}) copy-start(f32[512,448]{0,1:T(8,128)} %param.6) | copy-start | bytes 2752516
  83.5 16.9 %copy-start = (f32[512,448]{0,1:T(8,128)S(1)}, f32[512,448]{0,1:T(8,128)}, u32[]{:S(2)}) copy-start(f32[512,448]{0,1:T(8,128)} %param.8) | copy-start | bytes 2752516
  83.5 16.9 %copy-start.1 = (f32[512,448]{0,1:T(8,128)S(1)}, f32[512,448]{0,1:T(8,128)}, u32[]{:S(2)}) copy-start(f32[512,448]{0,1:T(8,128)} %param.9) | copy-start | bytes 2752516

commit v7 on v6

--- a/solution.py
+++ b/solution.py
@@ -8,10 +8,10 @@
 STEP = 100
 CORR_ONE = 1.0 - 0.9**STEP
 CORR_TWO = 1.0 - 0.999**STEP
-SPLIT = (("x", 4), ("pair", 2), ("near", 2), ("y", 8), ("zh", 4), ("core", 2))
+SPLIT = (("x", 4), ("pair", 2), ("near", 2), ("yfour", 4), ("ynear", 2), ("zh", 4), ("core", 2))
 ROW = ("x", "pair", "near")
 NEAR = ("x", "near")
-COL = ("y", "zh", "core")
+COL = ("yfour", "ynear", "zh", "core")
 VMEM = pl.BlockSpec(memory_space=pltpu.VMEM)
 SMEM = pl.BlockSpec(memory_space=pltpu.SMEM)
 HBM = pl.BlockSpec(memory_space=pl.ANY)
@@ -136,7 +136,10 @@
 def body(gradient, weight, projector, first_moment, second_moment):
     share = projector.shape[1]
     depth = projector.shape[0]
-    mine = gather(lax.all_gather(projector.T, "zh"), "y").reshape(-1, share, depth)
+    mine = projector.T
+    for axis in ("zh", "ynear", "yfour"):
+        mine = lax.all_gather(mine, axis)
+    mine = mine.reshape(-1, share, depth)
     other = lax.ppermute(mine, "core", [(0, 1), (1, 0)])
     core = lax.axis_index("core").astype(jnp.int32).reshape(1)
     grad = halve(gradient.T, mine)

time: 103 us -> 106 us (1.029)
  blocking collectives: 89.4 us -> 90.6 us
  starting transfers between devices: 7.35 us -> 8.41 us
    all_gather x1 -> x3, blocking collectives: 27.8 us -> 48.7 us  [body(): mine = lax.all_gather(mine, axis)]
    all_to_all x3 -> x2, blocking collectives: 54.8 us -> 35.2 us  [exchange(): return lax.all_to_all(blocks, axis, 0, 0)]
where the time goes in v7:
time: 106 us; the launch traced here: 105 us
  blocking collectives  90.6 us (85%)
  starting transfers between devices  8.41 us (8%)
  Pallas kernels  3.41 us (3%)
  waiting for transfers between devices  1.37 us (1%)
    all_gather x3, blocking collectives, body(): mine = lax.all_gather(mine, axis)  48.7 us
    all_to_all x2, blocking collectives, exchange(): return lax.all_to_all(blocks, axis, 0, 0)  35.2 us
    ppermute x1, starting transfers between devices, body(): other = lax.ppermute(mine, 'core', [(0, 1), (1, 0)])  8.41 us
    all_gather x1, blocking collectives, body(): low = jnp.sum(lax.all_gather(low, 'pair'), 0)  6.76 us
    pallas_call x1, Pallas kernels, step(): pl.pallas_call(step_kernel, out_shape=(shape, shape, jax.ShapeDtypeStruct...  2.14 us
  transfers between devices with their start and end apart: 1, of which 1 were waited for; matrix products, arithmetic and copies ran while one was open for 0% of the time, Pallas kernels for 0%

profile of v7, /device:TPU:1, one launch (start us, length us, event | category | flops | bytes accessed | tf_op | source)
XLA Modules:
  0.0 104.8 jit_solution(16721933354894181954)
XLA Ops:
  0.6 0.0 copy-start.3
  0.6 27.8 %all-gather = f32[32,512]{1,0:T(8,128)S(1)} all-gather(f32[8,512]{1,0:T(8,128)} %bitcast.23), channel_id=2, replica_groups=mesh['x'=4,'pair'=2,'near'=2,'yfour'=4,'ynear'=2,'zh'=4,'core'=2] {'zh'}, dimensions={0}, use_global_device_ids=true | all-gather | bytes 81920 | tf_op jit(solution)/shard_map/all_gather | solution.py:141
  28.4 3.8 %all-gather.1 = f32[8,8,512]{2,1,0:T(8,128)S(1)} all-gather(f32[4,8,512]{2,1,0:T(8,128)S(1)} %bitcast.22), channel_id=3, replica_groups=mesh['x'=4,'pair'=2,'near'=2,'yfour'=4,'ynear'=2,'zh'=4,'core'=2] {'ynear'}, dimensions={0}, use_global_device_ids=true | all-gather | bytes 196608 | tf_op jit(solution)/shard_map/all_gather | solution.py:141
  32.2 17.1 %all-gather.2 = f32[8,4,8,512]{3,2,1,0:T(8,128)S(1)} all-gather(f32[2,4,8,512]{3,2,1,0:T(8,128)S(1)} %bitcast.21), channel_id=4, replica_groups=mesh['x'=4,'pair'=2,'near'=2,'yfour'=4,'ynear'=2,'zh'=4,'core'=2] {'yfour'}, dimensions={0}, use_global_device_ids=true | all-gather | bytes 655360 | tf_op jit(solution)/shard_map/all_gather | solution.py:141
  49.4 8.4 %collective-permute-start = (f32[32,8,512]{2,1,0:T(8,128)S(1)}, f32[32,8,512]{2,1,0:T(8,128)S(1)}, u32[]{:S(2)}, u32[]{:S(2)}) collective-permute-start(f32[32,8,512]{2,1,0:T(8,128)S(1)} %bitcast.13), channel_id=1, source_target_pairs={{0,1},{1,0},{2,3},{3,2},{4,5},{5,4},{6,7},{7,6},{8,9},{9,8},{10,11... | collective-permute-start | bytes 1572872 | tf_op jit(solution)/shard_map/ppermute | solution.py:143
  57.8 0.0 copy-done.3
  57.8 0.1 halve.1
  57.9 1.4 %collective-permute-done.other_ref = f32[32,8,512]{2,1,0:T(8,128)S(1)} collective-permute-done((f32[32,8,512]{2,1,0:T(8,128)S(1)}, f32[32,8,512]{2,1,0:T(8,128)S(1)}, u32[]{:S(2)}, u32[]{:S(2)}) %collective-permute-start) | collective-permute-done | bytes 524320 | tf_op jit(solution)/shard_map/ppermute | solution.py:143
  59.3 1.1 %project.1 = (f32[8,56,512]{2,1,0:T(8,128)S(1)}, bf16[512,512]{1,0:T(8,128)(2,1)S(1)}, bf16[512,512]{1,0:T(8,128)(2,1)S(1)}) custom-call(s32[1]{0:T(128)} %bitcast.core_ref, f32[32,8,512]{2,1,0:T(8,128)S(1)} %bitcast.15, f32[32,8,512]{2,1,0:T(8,128)S(1)} %collective-permute-done.other_ref, bf16[448,512]{1,0:T(8,128)(2,1)S(1)} %get-tuple-element.11.grad_high_ref, ...), custom_call_target="tpu_custom_call" | custom-call | tf_op jit(solution)/shard_map/project/pallas_call | solution.py:98
  60.4 18.2 %all_to_all.10 = f32[8,56,512]{2,1,0:T(8,128)S(1)} all-to-all(f32[8,56,512]{2,1,0:T(8,128)S(1)} %get-tuple-element.13), channel_id=1, replica_groups=mesh['x'=4,'pair'=2,'near'=2,'yfour'=4,'ynear'=2,'zh'=4,'core'=2] {'x','..., dimensions={0} | all-to-all | bytes 1835008 | tf_op jit(solution)/shard_map/all_to_all | solution.py:129
  78.7 0.1 reduce_sum.18
  78.8 6.8 %all-gather.3 = f32[112,512]{1,0:T(8,128)S(1)} all-gather(f32[56,512]{1,0:T(8,128)S(1)} %reduce_sum.18), channel_id=5, replica_groups=mesh['x'=4,'pair'=2,'near'=2,'yfour'=4,'ynear'=2,'zh'=4,'core'=2] {'pair'}, dimensions={0}, use_global_device_ids=true | all-gather | bytes 344064 | tf_op jit(solution)/shard_map/all_gather | solution.py:149
  85.6 0.0 copy-start.2
  85.6 0.1 broadcast_in_dim.2
  85.7 0.0 copy-start
  85.7 0.0 copy-start.1
  85.7 16.9 %all_to_all.11.low_ref = f32[8,56,512]{2,1,0:T(8,128)S(1)} all-to-all(f32[8,56,512]{2,1,0:T(8,128)S(1)} %broadcast_in_dim.2), channel_id=1, replica_groups=mesh['x'=4,'pair'=2,'near'=2,'yfour'=4,'ynear'=2,'zh'=4,'core'=2] {'x','..., dimensions={0} | all-to-all | bytes 1835008 | tf_op jit(solution)/shard_map/all_to_all | solution.py:129
  102.6 0.0 copy-done.2
  102.6 0.0 copy-done
  102.6 0.0 copy-done.1
  102.6 2.1 %step.1 = (f32[448,512]{1,0:T(8,128)}, f32[448,512]{1,0:T(8,128)}, f32[448,512]{1,0:T(8,128)}) custom-call(f32[8,56,512]{2,1,0:T(8,128)S(1)} %all_to_all.11.low_ref, f32[448,512]{1,0:T(8,128)S(1)} %bitcast.16, f32[448,512]{1,0:T(8,128)S(1)} %bitcast.17, f32[448,512]{1,0:T(8,128)S(1)} %bitcast.18, bf16[512,512]{1,0:T(8,128)(2,1)S(1)} %get-tuple-element.14.high_ref, ...), custom_call_target="tpu_custom_call" | custom-call | tf_op jit(solution)/shard_map/step/pallas_call | solution.py:117
  (1 shorter events, 0.0 us)
Async XLA Ops:
  0.6 57.2 %copy-start.3 = (f32[512,448]{0,1:T(8,128)S(1)}, f32[512,448]{0,1:T(8,128)}, u32[]{:S(2)}) copy-start(f32[512,448]{0,1:T(8,128)} %param.5) | copy-start | bytes 2752516
  49.4 9.9 %collective-permute-start = (f32[32,8,512]{2,1,0:T(8,128)S(1)}, f32[32,8,512]{2,1,0:T(8,128)S(1)}, u32[]{:S(2)}, u32[]{:S(2)}) collective-permute-start(f32[32,8,512]{2,1,0:T(8,128)S(1)} %bitcast.13), channel_id=1, source_target_pairs={{0,1},{1,0},{2,3},{3,2},{4,5},{5,4},{6,7},{7,6},{8,9},{9,8},{10,11... | collective-permute-start | bytes 1572872 | tf_op jit(solution)/shard_map/ppermute | solution.py:143
  85.6 17.1 %copy-start.2 = (f32[512,448]{0,1:T(8,128)S(1)}, f32[512,448]{0,1:T(8,128)}, u32[]{:S(2)}) copy-start(f32[512,448]{0,1:T(8,128)} %param.6) | copy-start | bytes 2752516
  85.7 16.9 %copy-start = (f32[512,448]{0,1:T(8,128)S(1)}, f32[512,448]{0,1:T(8,128)}, u32[]{:S(2)}) copy-start(f32[512,448]{0,1:T(8,128)} %param.8) | copy-start | bytes 2752516
  85.7 16.9 %copy-start.1 = (f32[512,448]{0,1:T(8,128)S(1)}, f32[512,448]{0,1:T(8,128)}, u32[]{:S(2)}) copy-start(f32[512,448]{0,1:T(8,128)} %param.9) | copy-start | bytes 2752516

commit v8 on v6

--- a/solution.py
+++ b/solution.py
@@ -13,7 +13,6 @@
 NEAR = ("x", "near")
 COL = ("y", "zh", "core")
 VMEM = pl.BlockSpec(memory_space=pltpu.VMEM)
-SMEM = pl.BlockSpec(memory_space=pltpu.SMEM)
 HBM = pl.BlockSpec(memory_space=pl.ANY)
 PARAMS = pltpu.CompilerParams(vmem_limit_bytes=12 * 1024 * 1024)
 
@@ -37,12 +36,11 @@
 
 
 def project_kernel(
-    core_ref, mine_ref, other_ref, grad_high_ref, grad_rest_ref,
+    both_ref, grad_high_ref, grad_rest_ref,
     low_ref, high_ref, rest_hbm, order_ref, rest_ref, sem,
 ):
-    first = core_ref[0] == 0
-    order_ref[:, 0] = jnp.where(first, mine_ref[...], other_ref[...])
-    order_ref[:, 1] = jnp.where(first, other_ref[...], mine_ref[...])
+    order_ref[:, 0] = both_ref[0]
+    order_ref[:, 1] = both_ref[1]
     high, rest = split(order_ref[...].reshape(high_ref.shape))
     high_ref[...] = high
     rest_ref[...] = rest
@@ -91,23 +89,24 @@
     )(grad, after)
 
 
-def project(core, mine, other, grad, parts):
+def project(both, grad, parts):
     ff, depth = grad[0].shape
-    rank = mine.shape[0] * mine.shape[1] * 2
+    cores, blocks, share, _ = both.shape
+    rank = cores * blocks * share
     half = jax.ShapeDtypeStruct((rank, depth), jnp.bfloat16)
     return pl.pallas_call(
         project_kernel,
         out_shape=(jax.ShapeDtypeStruct((parts, ff // parts, rank), jnp.float32), half, half),
-        in_specs=[SMEM] + [VMEM] * 4,
+        in_specs=[VMEM] * 3,
         out_specs=(VMEM, VMEM, HBM),
         scratch_shapes=[
-            pltpu.VMEM((mine.shape[0], 2) + mine.shape[1:], jnp.float32),
+            pltpu.VMEM((blocks, cores, share, depth), jnp.float32),
             pltpu.VMEM((rank, depth), jnp.bfloat16),
             pltpu.SemaphoreType.DMA,
         ],
         compiler_params=PARAMS,
         name="project",
-    )(core, mine, other, *grad)
+    )(both, *grad)
 
 
 def step(low, first, second, weight, high, rest):
@@ -137,11 +136,10 @@
     share = projector.shape[1]
     depth = projector.shape[0]
     mine = gather(lax.all_gather(projector.T, "zh"), "y").reshape(-1, share, depth)
-    other = lax.ppermute(mine, "core", [(0, 1), (1, 0)])
-    core = lax.axis_index("core").astype(jnp.int32).reshape(1)
+    both = gather(mine, "core")
     grad = halve(gradient.T, mine)
     blocks = lax.axis_size(NEAR)
-    low, high, rest = project(core, mine, other, grad, blocks)
+    low, high, rest = project(both, grad, blocks)
     low = jnp.sum(exchange(low, NEAR), 0)
     low = jnp.sum(lax.all_gather(low, "pair"), 0)
     low = gather(low, NEAR)

time: 103 us -> 104 us (level)
  blocking collectives: 89.4 us -> 99 us
  starting transfers between devices: 7.35 us -> 0 us
  waiting for transfers between devices: 1.37 us -> 0 us
    all_to_all x3 -> x4, blocking collectives: 54.8 us -> 64.5 us  [exchange(): return lax.all_to_all(blocks, axis, 0, 0)]
    ppermute x1 -> x0, starting transfers between devices: 7.35 us -> none  [body(): other = lax.ppermute(mine, 'core', [(0, 1), (1, 0)])]
    ppermute x1 -> x0, waiting for transfers between devices: 1.37 us -> none  [body(): other = lax.ppermute(mine, 'core', [(0, 1), (1, 0)])]
  transfers between devices with their start and end apart: 1 -> 0, of which waited for: 1 -> 0; matrix products, arithmetic and copies ran while one was open for 0% -> 0% of each run, Pallas kernels for 0% -> 0%
where the time goes in v8:
time: 104 us; the launch traced here: 103 us
  blocking collectives  99 us (95%)
  Pallas kernels  3.34 us (3%)
    all_to_all x4, blocking collectives, exchange(): return lax.all_to_all(blocks, axis, 0, 0)  64.5 us
    all_gather x1, blocking collectives, body(): lax.all_gather(projector.T, 'zh')  27.8 us
    all_gather x1, blocking collectives, body(): low = jnp.sum(lax.all_gather(low, 'pair'), 0)  6.76 us
    pallas_call x1, Pallas kernels, step(): pl.pallas_call(step_kernel, out_shape=(shape, shape, jax.ShapeDtypeStruct...  2.14 us

profile of v8, /device:TPU:1, one launch (start us, length us, event | category | flops | bytes accessed | tf_op | source)
XLA Modules:
  0.0 103.5 jit_solution(9111543629970896820)
XLA Ops:
  0.6 0.0 copy-start.3
  0.6 27.8 %all-gather = f32[32,512]{1,0:T(8,128)S(1)} all-gather(f32[8,512]{1,0:T(8,128)} %bitcast.19), channel_id=2, replica_groups=mesh['x'=4,'pair'=2,'near'=2,'y'=8,'zh'=4,'core'=2] {'zh'}, dimensions={0}, use_global_device_ids=true | all-gather | bytes 81920 | tf_op jit(solution)/shard_map/all_gather | solution.py:138
  28.4 0.1 broadcast_in_dim.8
  28.5 19.7 %all_to_all.20 = f32[8,4,8,512]{3,2,1,0:T(8,128)S(1)} all-to-all(f32[8,4,8,512]{3,2,1,0:T(8,128)S(1)} %broadcast_in_dim.8), channel_id=1, replica_groups=mesh['x'=4,'pair'=2,'near'=2,'y'=8,'zh'=4,'core'=2] {'y'}, dimensions={0} | all-to-all | bytes 1048576 | tf_op jit(solution)/shard_map/all_to_all | solution.py:128
  48.2 0.0 copy-done.3
  48.2 0.1 halve.1
  48.3 0.1 broadcast_in_dim.10
  48.5 9.7 %all_to_all.21.both_ref = f32[2,32,8,512]{3,2,1,0:T(8,128)S(1)} all-to-all(f32[2,32,8,512]{3,2,1,0:T(8,128)S(1)} %broadcast_in_dim.10), channel_id=1, replica_groups=mesh['x'=4,'pair'=2,'near'=2,'y'=8,'zh'=4,'core'=2] {'core'}, dimensions={0} | all-to-all | bytes 2097152 | tf_op jit(solution)/shard_map/all_to_all | solution.py:128
  58.1 1.1 %project.1 = (f32[8,56,512]{2,1,0:T(8,128)S(1)}, bf16[512,512]{1,0:T(8,128)(2,1)S(1)}, bf16[512,512]{1,0:T(8,128)(2,1)S(1)}) custom-call(f32[2,32,8,512]{3,2,1,0:T(8,128)S(1)} %all_to_all.21.both_ref, bf16[448,512]{1,0:T(8,128)(2,1)S(1)} %get-tuple-element.11.grad_high_ref, bf16[448,512]{1,0:T(8,128)(2,1)S(1)} %get-tuple-element.12.grad_rest_ref), custom_call_target="tpu_custom_call" | custom-call | tf_op jit(solution)/shard_map/project/pallas_call | solution.py:97
  59.2 18.2 %all_to_all.22 = f32[8,56,512]{2,1,0:T(8,128)S(1)} all-to-all(f32[8,56,512]{2,1,0:T(8,128)S(1)} %get-tuple-element.13), channel_id=1, replica_groups=mesh['x'=4,'pair'=2,'near'=2,'y'=8,'zh'=4,'core'=2] {'x','near'}, dimensions={0} | all-to-all | bytes 1835008 | tf_op jit(solution)/shard_map/all_to_all | solution.py:128
  77.5 0.1 reduce_sum.18
  77.6 6.8 %all-gather.1 = f32[112,512]{1,0:T(8,128)S(1)} all-gather(f32[56,512]{1,0:T(8,128)S(1)} %reduce_sum.18), channel_id=3, replica_groups=mesh['x'=4,'pair'=2,'near'=2,'y'=8,'zh'=4,'core'=2] {'pair'}, dimensions={0}, use_global_device_ids=true | all-gather | bytes 344064 | tf_op jit(solution)/shard_map/all_gather | solution.py:144
  84.3 0.0 copy-start.2
  84.4 0.1 broadcast_in_dim.22
  84.5 0.0 copy-start
  84.5 0.0 copy-start.1
  84.5 16.9 %all_to_all.23.low_ref = f32[8,56,512]{2,1,0:T(8,128)S(1)} all-to-all(f32[8,56,512]{2,1,0:T(8,128)S(1)} %broadcast_in_dim.22), channel_id=1, replica_groups=mesh['x'=4,'pair'=2,'near'=2,'y'=8,'zh'=4,'core'=2] {'x','near'}, dimensions={0} | all-to-all | bytes 1835008 | tf_op jit(solution)/shard_map/all_to_all | solution.py:128
  101.3 0.0 copy-done.2
  101.3 0.0 copy-done
  101.3 0.0 copy-done.1
  101.3 2.1 %step.1 = (f32[448,512]{1,0:T(8,128)}, f32[448,512]{1,0:T(8,128)}, f32[448,512]{1,0:T(8,128)}) custom-call(f32[8,56,512]{2,1,0:T(8,128)S(1)} %all_to_all.23.low_ref, f32[448,512]{1,0:T(8,128)S(1)} %bitcast.13, f32[448,512]{1,0:T(8,128)S(1)} %bitcast.14, f32[448,512]{1,0:T(8,128)S(1)} %bitcast.15, bf16[512,512]{1,0:T(8,128)(2,1)S(1)} %get-tuple-element.14.high_ref, ...), custom_call_target="tpu_custom_call" | custom-call | tf_op jit(solution)/shard_map/step/pallas_call | solution.py:116
  (1 shorter events, 0.0 us)
Async XLA Ops:
  0.6 47.6 %copy-start.3 = (f32[512,448]{0,1:T(8,128)S(1)}, f32[512,448]{0,1:T(8,128)}, u32[]{:S(2)}) copy-start(f32[512,448]{0,1:T(8,128)} %param.5) | copy-start | bytes 2752516
  84.3 17.0 %copy-start.2 = (f32[512,448]{0,1:T(8,128)S(1)}, f32[512,448]{0,1:T(8,128)}, u32[]{:S(2)}) copy-start(f32[512,448]{0,1:T(8,128)} %param.6) | copy-start | bytes 2752516
  84.5 16.9 %copy-start = (f32[512,448]{0,1:T(8,128)S(1)}, f32[512,448]{0,1:T(8,128)}, u32[]{:S(2)}) copy-start(f32[512,448]{0,1:T(8,128)} %param.8) | copy-start | bytes 2752516
  84.5 16.9 %copy-start.1 = (f32[512,448]{0,1:T(8,128)S(1)}, f32[512,448]{0,1:T(8,128)}, u32[]{:S(2)}) copy-start(f32[512,448]{0,1:T(8,128)} %param.9) | copy-start | bytes 2752516

commit v9 on v6

--- a/solution.py
+++ b/solution.py
@@ -10,7 +10,7 @@
 CORR_TWO = 1.0 - 0.999**STEP
 SPLIT = (("x", 4), ("pair", 2), ("near", 2), ("y", 8), ("zh", 4), ("core", 2))
 ROW = ("x", "pair", "near")
-NEAR = ("x", "near")
+NEAR = ("near", "x")
 COL = ("y", "zh", "core")
 VMEM = pl.BlockSpec(memory_space=pltpu.VMEM)
 SMEM = pl.BlockSpec(memory_space=pltpu.SMEM)

time: 103 us -> 103 us (level)
    all_to_all x3, blocking collectives: 54.8 us -> 53.8 us  [exchange(): return lax.all_to_all(blocks, axis, 0, 0)]
where the time goes in v9:
time: 103 us; the launch traced here: 102 us
  blocking collectives  88.4 us (86%)
  starting transfers between devices  7.35 us (7%)
  Pallas kernels  3.41 us (3%)
  waiting for transfers between devices  1.37 us (1%)
    all_to_all x3, blocking collectives, exchange(): return lax.all_to_all(blocks, axis, 0, 0)  53.8 us
    all_gather x1, blocking collectives, body(): lax.all_gather(projector.T, 'zh')  27.8 us
    ppermute x1, starting transfers between devices, body(): other = lax.ppermute(mine, 'core', [(0, 1), (1, 0)])  7.35 us
    all_gather x1, blocking collectives, body(): low = jnp.sum(lax.all_gather(low, 'pair'), 0)  6.81 us
    pallas_call x1, Pallas kernels, step(): pl.pallas_call(step_kernel, out_shape=(shape, shape, jax.ShapeDtypeStruct...  2.14 us
  transfers between devices with their start and end apart: 1, of which 1 were waited for; matrix products, arithmetic and copies ran while one was open for 0% of the time, Pallas kernels for 0%

profile of v9, /device:TPU:1, one launch (start us, length us, event | category | flops | bytes accessed | tf_op | source)
XLA Modules:
  0.0 101.5 jit_solution(9520881089357678692)
XLA Ops:
  0.6 0.0 copy-start.3
  0.6 27.8 %all-gather = f32[32,512]{1,0:T(8,128)S(1)} all-gather(f32[8,512]{1,0:T(8,128)} %bitcast.21), channel_id=2, replica_groups=mesh['x'=4,'pair'=2,'near'=2,'y'=8,'zh'=4,'core'=2] {'zh'}, dimensions={0}, use_global_device_ids=true | all-gather | bytes 81920 | tf_op jit(solution)/shard_map/all_gather | solution.py:139
  28.4 0.1 broadcast_in_dim.4
  28.5 19.7 %all_to_all.15 = f32[8,4,8,512]{3,2,1,0:T(8,128)S(1)} all-to-all(f32[8,4,8,512]{3,2,1,0:T(8,128)S(1)} %broadcast_in_dim.4), channel_id=1, replica_groups=mesh['x'=4,'pair'=2,'near'=2,'y'=8,'zh'=4,'core'=2] {'y'}, dimensions={0} | all-to-all | bytes 1048576 | tf_op jit(solution)/shard_map/all_to_all | solution.py:129
  48.2 7.4 %collective-permute-start = (f32[32,8,512]{2,1,0:T(8,128)S(1)}, f32[32,8,512]{2,1,0:T(8,128)S(1)}, u32[]{:S(2)}, u32[]{:S(2)}) collective-permute-start(f32[32,8,512]{2,1,0:T(8,128)S(1)} %bitcast.12), channel_id=1, source_target_pairs={{0,1},{1,0},{2,3},{3,2},{4,5},{5,4},{6,7},{7,6},{8,9},{9,8},{10,11... | collective-permute-start | bytes 1572872 | tf_op jit(solution)/shard_map/ppermute | solution.py:140
  55.6 0.0 copy-done.3
  55.6 0.1 halve.1
  55.7 1.4 %collective-permute-done.other_ref = f32[32,8,512]{2,1,0:T(8,128)S(1)} collective-permute-done((f32[32,8,512]{2,1,0:T(8,128)S(1)}, f32[32,8,512]{2,1,0:T(8,128)S(1)}, u32[]{:S(2)}, u32[]{:S(2)}) %collective-permute-start) | collective-permute-done | bytes 524320 | tf_op jit(solution)/shard_map/ppermute | solution.py:140
  57.1 1.2 %project.1 = (f32[8,56,512]{2,1,0:T(8,128)S(1)}, bf16[512,512]{1,0:T(8,128)(2,1)S(1)}, bf16[512,512]{1,0:T(8,128)(2,1)S(1)}) custom-call(s32[1]{0:T(128)} %bitcast.core_ref, f32[32,8,512]{2,1,0:T(8,128)S(1)} %bitcast.14, f32[32,8,512]{2,1,0:T(8,128)S(1)} %collective-permute-done.other_ref, bf16[448,512]{1,0:T(8,128)(2,1)S(1)} %get-tuple-element.11.grad_high_ref, ...), custom_call_target="tpu_custom_call" | custom-call | tf_op jit(solution)/shard_map/project/pallas_call | solution.py:98
  58.3 18.2 %all_to_all.16 = f32[8,56,512]{2,1,0:T(8,128)S(1)} all-to-all(f32[8,56,512]{2,1,0:T(8,128)S(1)} %get-tuple-element.13), channel_id=1, replica_groups=mesh['x'=4,'pair'=2,'near'=2,'y'=8,'zh'=4,'core'=2] {'near','x'}, dimensions={0} | all-to-all | bytes 1835008 | tf_op jit(solution)/shard_map/all_to_all | solution.py:129
  76.4 0.1 reduce_sum.18
  76.5 6.8 %all-gather.1 = f32[112,512]{1,0:T(8,128)S(1)} all-gather(f32[56,512]{1,0:T(8,128)S(1)} %reduce_sum.18), channel_id=3, replica_groups=mesh['x'=4,'pair'=2,'near'=2,'y'=8,'zh'=4,'core'=2] {'pair'}, dimensions={0}, use_global_device_ids=true | all-gather | bytes 344064 | tf_op jit(solution)/shard_map/all_gather | solution.py:146
  83.3 0.0 copy-start.2
  83.3 0.1 broadcast_in_dim.5
  83.4 0.0 copy-start
  83.5 0.0 copy-start.1
  83.5 15.9 %all_to_all.17.low_ref = f32[8,56,512]{2,1,0:T(8,128)S(1)} all-to-all(f32[8,56,512]{2,1,0:T(8,128)S(1)} %broadcast_in_dim.5), channel_id=1, replica_groups=mesh['x'=4,'pair'=2,'near'=2,'y'=8,'zh'=4,'core'=2] {'near','x'}, dimensions={0} | all-to-all | bytes 1835008 | tf_op jit(solution)/shard_map/all_to_all | solution.py:129
  99.4 0.0 copy-done.2
  99.4 0.0 copy-done
  99.4 0.0 copy-done.1
  99.4 2.1 %step.1 = (f32[448,512]{1,0:T(8,128)}, f32[448,512]{1,0:T(8,128)}, f32[448,512]{1,0:T(8,128)}) custom-call(f32[8,56,512]{2,1,0:T(8,128)S(1)} %all_to_all.17.low_ref, f32[448,512]{1,0:T(8,128)S(1)} %bitcast.15, f32[448,512]{1,0:T(8,128)S(1)} %bitcast.16, f32[448,512]{1,0:T(8,128)S(1)} %bitcast.17, bf16[512,512]{1,0:T(8,128)(2,1)S(1)} %get-tuple-element.14.high_ref, ...), custom_call_target="tpu_custom_call" | custom-call | tf_op jit(solution)/shard_map/step/pallas_call | solution.py:117
  (1 shorter events, 0.0 us)
Async XLA Ops:
  0.6 55.0 %copy-start.3 = (f32[512,448]{0,1:T(8,128)S(1)}, f32[512,448]{0,1:T(8,128)}, u32[]{:S(2)}) copy-start(f32[512,448]{0,1:T(8,128)} %param.5) | copy-start | bytes 2752516
  48.2 8.9 %collective-permute-start = (f32[32,8,512]{2,1,0:T(8,128)S(1)}, f32[32,8,512]{2,1,0:T(8,128)S(1)}, u32[]{:S(2)}, u32[]{:S(2)}) collective-permute-start(f32[32,8,512]{2,1,0:T(8,128)S(1)} %bitcast.12), channel_id=1, source_target_pairs={{0,1},{1,0},{2,3},{3,2},{4,5},{5,4},{6,7},{7,6},{8,9},{9,8},{10,11... | collective-permute-start | bytes 1572872 | tf_op jit(solution)/shard_map/ppermute | solution.py:140
  83.3 16.0 %copy-start.2 = (f32[512,448]{0,1:T(8,128)S(1)}, f32[512,448]{0,1:T(8,128)}, u32[]{:S(2)}) copy-start(f32[512,448]{0,1:T(8,128)} %param.6) | copy-start | bytes 2752516
  83.4 15.9 %copy-start = (f32[512,448]{0,1:T(8,128)S(1)}, f32[512,448]{0,1:T(8,128)}, u32[]{:S(2)}) copy-start(f32[512,448]{0,1:T(8,128)} %param.8) | copy-start | bytes 2752516
  83.5 15.9 %copy-start.1 = (f32[512,448]{0,1:T(8,128)S(1)}, f32[512,448]{0,1:T(8,128)}, u32[]{:S(2)}) copy-start(f32[512,448]{0,1:T(8,128)} %param.9) | copy-start | bytes 2752516

commit v10 on v9

--- a/solution.py
+++ b/solution.py
@@ -8,10 +8,11 @@
 STEP = 100
 CORR_ONE = 1.0 - 0.9**STEP
 CORR_TWO = 1.0 - 0.999**STEP
-SPLIT = (("x", 4), ("pair", 2), ("near", 2), ("y", 8), ("zh", 4), ("core", 2))
+SPLIT = (("x", 4), ("pair", 2), ("near", 2), ("yfour", 4), ("ynear", 2), ("zh", 4), ("core", 2))
 ROW = ("x", "pair", "near")
 NEAR = ("near", "x")
-COL = ("y", "zh", "core")
+COL = ("yfour", "ynear", "zh", "core")
+Y = ("ynear", "yfour")
 VMEM = pl.BlockSpec(memory_space=pltpu.VMEM)
 SMEM = pl.BlockSpec(memory_space=pltpu.SMEM)
 HBM = pl.BlockSpec(memory_space=pl.ANY)
@@ -41,8 +42,9 @@
     low_ref, high_ref, rest_hbm, order_ref, rest_ref, sem,
 ):
     first = core_ref[0] == 0
-    order_ref[:, 0] = jnp.where(first, mine_ref[...], other_ref[...])
-    order_ref[:, 1] = jnp.where(first, other_ref[...], mine_ref[...])
+    for i in range(mine_ref.shape[0]):
+        order_ref[:, i, :, 0] = jnp.where(first, mine_ref[i], other_ref[i])
+        order_ref[:, i, :, 1] = jnp.where(first, other_ref[i], mine_ref[i])
     high, rest = split(order_ref[...].reshape(high_ref.shape))
     high_ref[...] = high
     rest_ref[...] = rest
@@ -93,7 +95,8 @@
 
 def project(core, mine, other, grad, parts):
     ff, depth = grad[0].shape
-    rank = mine.shape[0] * mine.shape[1] * 2
+    near, four, zh, share, _ = mine.shape
+    rank = near * four * zh * 2 * share
     half = jax.ShapeDtypeStruct((rank, depth), jnp.bfloat16)
     return pl.pallas_call(
         project_kernel,
@@ -101,7 +104,7 @@
         in_specs=[SMEM] + [VMEM] * 4,
         out_specs=(VMEM, VMEM, HBM),
         scratch_shapes=[
-            pltpu.VMEM((mine.shape[0], 2) + mine.shape[1:], jnp.float32),
+            pltpu.VMEM((four, near, zh, 2, share, depth), jnp.float32),
             pltpu.VMEM((rank, depth), jnp.bfloat16),
             pltpu.SemaphoreType.DMA,
         ],
@@ -136,7 +139,8 @@
 def body(gradient, weight, projector, first_moment, second_moment):
     share = projector.shape[1]
     depth = projector.shape[0]
-    mine = gather(lax.all_gather(projector.T, "zh"), "y").reshape(-1, share, depth)
+    mine = gather(lax.all_gather(projector.T, "zh"), Y)
+    mine = mine.reshape(lax.axis_size("ynear"), lax.axis_size("yfour"), -1, share, depth)
     other = lax.ppermute(mine, "core", [(0, 1), (1, 0)])
     core = lax.axis_index("core").astype(jnp.int32).reshape(1)
     grad = halve(gradient.T, mine)

time: 103 us -> 102 us (level)
  the two profiles are of different devices: /device:TPU:1 before, /device:TPU:8 now
where the time goes in v10:
time: 102 us
  blocking collectives  94 us (92%)
  Pallas kernels  3.41 us (3%)
  starting transfers between devices  1.91 us (2%)
  waiting for transfers between devices  1.73 us (2%)
    all_to_all x3, blocking collectives, exchange(): return lax.all_to_all(blocks, axis, 0, 0)  56.6 us
    all_gather x1, blocking collectives, body(): mine = gather(lax.all_gather(projector.T, 'zh'), Y)  29.7 us
    all_gather x1, blocking collectives, body(): low = jnp.sum(lax.all_gather(low, 'pair'), 0)  7.72 us
    pallas_call x1, Pallas kernels, step(): pl.pallas_call(step_kernel, out_shape=(shape, shape, jax.ShapeDtypeStruct...  2.13 us
  transfers between devices with their start and end apart: 1, of which 1 were waited for; matrix products, arithmetic and copies ran while one was open for 0% of the time, Pallas kernels for 0%

profile of v10, /device:TPU:8, one launch (start us, length us, event | category | flops | bytes accessed | tf_op | source)
XLA Modules:
  0.0 102.0 jit_solution(12491791919306996474)
XLA Ops:
  0.6 0.0 copy-start.3
  0.6 29.7 %all-gather = f32[32,512]{1,0:T(8,128)S(1)} all-gather(f32[8,512]{1,0:T(8,128)} %bitcast.21), channel_id=2, replica_groups=mesh['x'=4,'pair'=2,'near'=2,'yfour'=4,'ynear'=2,'zh'=4,'core'=2] {'zh'}, dimensions={0}, use_global_device_ids=true | all-gather | bytes 81920 | tf_op jit(solution)/shard_map/all_gather | solution.py:142
  30.4 20.7 %all_to_all.15 = f32[8,4,8,512]{3,2,1,0:T(8,128)S(1)} all-to-all(f32[8,4,8,512]{3,2,1,0:T(8,128)S(1)} %broadcast_in_dim.4), channel_id=1, replica_groups=mesh['x'=4,'pair'=2,'near'=2,'yfour'=4,'ynear'=2,'zh'=4,'core'=2] {'ynea..., dimensions={0} | all-to-all | bytes 1048576 | tf_op jit(solution)/shard_map/all_to_all | solution.py:132
  51.2 1.9 %collective-permute-start = (f32[2,4,4,8,512]{4,3,2,1,0:T(8,128)S(1)}, f32[2,4,4,8,512]{4,3,2,1,0:T(8,128)S(1)}, u32[]{:S(2)}, u32[]{:S(2)}) collective-permute-start(f32[2,4,4,8,512]{4,3,2,1,0:T(8,128)S(1)} %bitcast.12), channel_id=1, source_target_pairs={{0,1},{1,0},{2,3},{3,2},{4,5},{5,4},{6,7},{7,6},{8,9},{9,8},{10,11... | collective-permute-start | bytes 1572872 | tf_op jit(solution)/shard_map/ppermute | solution.py:144
  53.1 0.0 copy-done.3
  53.1 0.1 halve.1
  53.2 1.7 %collective-permute-done.other_ref = f32[2,4,4,8,512]{4,3,2,1,0:T(8,128)S(1)} collective-permute-done((f32[2,4,4,8,512]{4,3,2,1,0:T(8,128)S(1)}, f32[2,4,4,8,512]{4,3,2,1,0:T(8,128)S(1)}, u32[]{:S(2)}, u32[]{:S(2)}) %collective-permute-start) | collective-permute-done | bytes 524320 | tf_op jit(solution)/shard_map/ppermute | solution.py:144
  54.9 1.2 %project.1 = (f32[8,56,512]{2,1,0:T(8,128)S(1)}, bf16[512,512]{1,0:T(8,128)(2,1)S(1)}, bf16[512,512]{1,0:T(8,128)(2,1)S(1)}) custom-call(s32[1]{0:T(128)} %bitcast.core_ref, f32[2,4,4,8,512]{4,3,2,1,0:T(8,128)S(1)} %bitcast.14, f32[2,4,4,8,512]{4,3,2,1,0:T(8,128)S(1)} %collective-permute-done.other_ref, ...), custom_call_target="tpu_custom_call" | custom-call | tf_op jit(solution)/shard_map/project/pallas_call | solution.py:101
  56.1 19.7 %all_to_all.16 = f32[8,56,512]{2,1,0:T(8,128)S(1)} all-to-all(f32[8,56,512]{2,1,0:T(8,128)S(1)} %get-tuple-element.13), channel_id=1, replica_groups=mesh['x'=4,'pair'=2,'near'=2,'yfour'=4,'ynear'=2,'zh'=4,'core'=2] {'near..., dimensions={0} | all-to-all | bytes 1835008 | tf_op jit(solution)/shard_map/all_to_all | solution.py:132
  75.8 0.1 reduce_sum.18
  75.8 7.7 %all-gather.1 = f32[112,512]{1,0:T(8,128)S(1)} all-gather(f32[56,512]{1,0:T(8,128)S(1)} %reduce_sum.18), channel_id=3, replica_groups=mesh['x'=4,'pair'=2,'near'=2,'yfour'=4,'ynear'=2,'zh'=4,'core'=2] {'pair'}, dimensions={0}, use_global_device_ids=true | all-gather | bytes 344064 | tf_op jit(solution)/shard_map/all_gather | solution.py:150
  83.6 0.0 copy-start.2
  83.6 0.1 broadcast_in_dim.5
  83.7 0.0 copy-start
  83.7 0.0 copy-start.1
  83.7 16.2 %all_to_all.17.low_ref = f32[8,56,512]{2,1,0:T(8,128)S(1)} all-to-all(f32[8,56,512]{2,1,0:T(8,128)S(1)} %broadcast_in_dim.5), channel_id=1, replica_groups=mesh['x'=4,'pair'=2,'near'=2,'yfour'=4,'ynear'=2,'zh'=4,'core'=2] {'near..., dimensions={0} | all-to-all | bytes 1835008 | tf_op jit(solution)/shard_map/all_to_all | solution.py:132
  99.9 0.0 copy-done.2
  99.9 0.0 copy-done
  99.9 0.0 copy-done.1
  99.9 2.1 %step.1 = (f32[448,512]{1,0:T(8,128)}, f32[448,512]{1,0:T(8,128)}, f32[448,512]{1,0:T(8,128)}) custom-call(f32[8,56,512]{2,1,0:T(8,128)S(1)} %all_to_all.17.low_ref, f32[448,512]{1,0:T(8,128)S(1)} %bitcast.15, f32[448,512]{1,0:T(8,128)S(1)} %bitcast.16, f32[448,512]{1,0:T(8,128)S(1)} %bitcast.17, bf16[512,512]{1,0:T(8,128)(2,1)S(1)} %get-tuple-element.14.high_ref, ...), custom_call_target="tpu_custom_call" | custom-call | tf_op jit(solution)/shard_map/step/pallas_call | solution.py:120
  (2 shorter events, 0.1 us)
Async XLA Ops:
  0.6 52.4 %copy-start.3 = (f32[512,448]{0,1:T(8,128)S(1)}, f32[512,448]{0,1:T(8,128)}, u32[]{:S(2)}) copy-start(f32[512,448]{0,1:T(8,128)} %param.5) | copy-start | bytes 2752516
  51.2 3.8 %collective-permute-start = (f32[2,4,4,8,512]{4,3,2,1,0:T(8,128)S(1)}, f32[2,4,4,8,512]{4,3,2,1,0:T(8,128)S(1)}, u32[]{:S(2)}, u32[]{:S(2)}) collective-permute-start(f32[2,4,4,8,512]{4,3,2,1,0:T(8,128)S(1)} %bitcast.12), channel_id=1, source_target_pairs={{0,1},{1,0},{2,3},{3,2},{4,5},{5,4},{6,7},{7,6},{8,9},{9,8},{10,11... | collective-permute-start | bytes 1572872 | tf_op jit(solution)/shard_map/ppermute | solution.py:144
  83.6 16.3 %copy-start.2 = (f32[512,448]{0,1:T(8,128)S(1)}, f32[512,448]{0,1:T(8,128)}, u32[]{:S(2)}) copy-start(f32[512,448]{0,1:T(8,128)} %param.6) | copy-start | bytes 2752516
  83.7 16.2 %copy-start = (f32[512,448]{0,1:T(8,128)S(1)}, f32[512,448]{0,1:T(8,128)}, u32[]{:S(2)}) copy-start(f32[512,448]{0,1:T(8,128)} %param.8) | copy-start | bytes 2752516
  83.7 16.2 %copy-start.1 = (f32[512,448]{0,1:T(8,128)S(1)}, f32[512,448]{0,1:T(8,128)}, u32[]{:S(2)}) copy-start(f32[512,448]{0,1:T(8,128)} %param.9) | copy-start | bytes 2752516

commit v11 on v10

--- a/solution.py
+++ b/solution.py
@@ -8,11 +8,11 @@
 STEP = 100
 CORR_ONE = 1.0 - 0.9**STEP
 CORR_TWO = 1.0 - 0.999**STEP
-SPLIT = (("x", 4), ("pair", 2), ("near", 2), ("yfour", 4), ("ynear", 2), ("zh", 4), ("core", 2))
+SPLIT = (("x", 4), ("pair", 2), ("near", 2), ("yfar", 2), ("ymid", 2), ("ynear", 2), ("zh", 4), ("core", 2))
 ROW = ("x", "pair", "near")
 NEAR = ("near", "x")
-COL = ("yfour", "ynear", "zh", "core")
-Y = ("ynear", "yfour")
+COL = ("yfar", "ymid", "ynear", "zh", "core")
+Y = ("ynear", "ymid", "yfar")
 VMEM = pl.BlockSpec(memory_space=pltpu.VMEM)
 SMEM = pl.BlockSpec(memory_space=pltpu.SMEM)
 HBM = pl.BlockSpec(memory_space=pl.ANY)
@@ -43,8 +43,9 @@
 ):
     first = core_ref[0] == 0
     for i in range(mine_ref.shape[0]):
-        order_ref[:, i, :, 0] = jnp.where(first, mine_ref[i], other_ref[i])
-        order_ref[:, i, :, 1] = jnp.where(first, other_ref[i], mine_ref[i])
+        for j in range(mine_ref.shape[1]):
+            order_ref[:, j, i, :, 0] = jnp.where(first, mine_ref[i, j], other_ref[i, j])
+            order_ref[:, j, i, :, 1] = jnp.where(first, other_ref[i, j], mine_ref[i, j])
     high, rest = split(order_ref[...].reshape(high_ref.shape))
     high_ref[...] = high
     rest_ref[...] = rest
@@ -95,8 +96,8 @@
 
 def project(core, mine, other, grad, parts):
     ff, depth = grad[0].shape
-    near, four, zh, share, _ = mine.shape
-    rank = near * four * zh * 2 * share
+    near, mid, far, zh, share, _ = mine.shape
+    rank = near * mid * far * zh * 2 * share
     half = jax.ShapeDtypeStruct((rank, depth), jnp.bfloat16)
     return pl.pallas_call(
         project_kernel,
@@ -104,7 +105,7 @@
         in_specs=[SMEM] + [VMEM] * 4,
         out_specs=(VMEM, VMEM, HBM),
         scratch_shapes=[
-            pltpu.VMEM((four, near, zh, 2, share, depth), jnp.float32),
+            pltpu.VMEM((far, mid, near, zh, 2, share, depth), jnp.float32),
             pltpu.VMEM((rank, depth), jnp.bfloat16),
             pltpu.SemaphoreType.DMA,
         ],
@@ -140,7 +141,7 @@
     share = projector.shape[1]
     depth = projector.shape[0]
     mine = gather(lax.all_gather(projector.T, "zh"), Y)
-    mine = mine.reshape(lax.axis_size("ynear"), lax.axis_size("yfour"), -1, share, depth)
+    mine = mine.reshape(tuple(lax.axis_size(axis) for axis in Y) + (-1, share, depth))
     other = lax.ppermute(mine, "core", [(0, 1), (1, 0)])
     core = lax.axis_index("core").astype(jnp.int32).reshape(1)
     grad = halve(gradient.T, mine)

time: 102 us -> 101 us (level)
  the two profiles are of different devices: /device:TPU:8 before, /device:TPU:16 now
where the time goes in v11:
time: 101 us
  blocking collectives  93 us (92%)
  Pallas kernels  3.41 us (3%)
  starting transfers between devices  1.91 us (2%)
  waiting for transfers between devices  1.73 us (2%)
    all_to_all x3, blocking collectives, exchange(): return lax.all_to_all(blocks, axis, 0, 0)  55.6 us
    all_gather x1, blocking collectives, body(): mine = gather(lax.all_gather(projector.T, 'zh'), Y)  29.7 us
    all_gather x1, blocking collectives, body(): low = jnp.sum(lax.all_gather(low, 'pair'), 0)  7.71 us
    pallas_call x1, Pallas kernels, step(): pl.pallas_call(step_kernel, out_shape=(shape, shape, jax.ShapeDtypeStruct...  2.13 us
  transfers between devices with their start and end apart: 1, of which 1 were waited for; matrix products, arithmetic and copies ran while one was open for 0% of the time, Pallas kernels for 0%

profile of v11, /device:TPU:16, one launch (start us, length us, event | category | flops | bytes accessed | tf_op | source)
XLA Modules:
  0.0 101.0 jit_solution(17420455808412005771)
XLA Ops:
  0.6 0.0 copy-start.3
  0.6 29.7 %all-gather = f32[32,512]{1,0:T(8,128)S(1)} all-gather(f32[8,512]{1,0:T(8,128)} %bitcast.21), channel_id=2, replica_groups=mesh['x'=4,'pair'=2,'near'=2,'yfar'=2,'ymid'=2,'ynear'=2,'zh'=4,'core'=2..., dimensions={0}, use_global_device_ids=true | all-gather | bytes 81920 | tf_op jit(solution)/shard_map/all_gather | solution.py:143
  30.4 19.7 %all_to_all.15 = f32[8,4,8,512]{3,2,1,0:T(8,128)S(1)} all-to-all(f32[8,4,8,512]{3,2,1,0:T(8,128)S(1)} %broadcast_in_dim.4), channel_id=1, replica_groups=mesh['x'=4,'pair'=2,'near'=2,'yfar'=2,'ymid'=2,'ynear'=2,'zh'=4,'core'=2..., dimensions={0} | all-to-all | bytes 1048576 | tf_op jit(solution)/shard_map/all_to_all | solution.py:133
  50.1 1.9 %collective-permute-start = (f32[2,2,2,4,8,512]{5,4,3,2,1,0:T(8,128)S(1)}, f32[2,2,2,4,8,512]{5,4,3,2,1,0:T(8,128)S(1)}, u32[]{:S(2)}, u32[]{:S(2)}) collective-permute-start(f32[2,2,2,4,8,512]{5,4,3,2,1,0:T(8,128)S(1)} %bitcast.12), channel_id=1, source_target_pairs={{0,1},{1,0},{2,3},{3,2},{4,5},{5,4},{6,7},{7,6},{8,9},{9,8},{10,11... | collective-permute-start | bytes 1572872 | tf_op jit(solution)/shard_map/ppermute | solution.py:145
  52.1 0.0 copy-done.3
  52.1 0.1 halve.1
  52.2 1.7 %collective-permute-done.other_ref = f32[2,2,2,4,8,512]{5,4,3,2,1,0:T(8,128)S(1)} collective-permute-done((f32[2,2,2,4,8,512]{5,4,3,2,1,0:T(8,128)S(1)}, f32[2,2,2,4,8,512]{5,4,3,2,1,0:T(8,128)S(1)}, u32[]{:S(2)}, u32[]{:S(2)}) %collective-permute-start) | collective-permute-done | bytes 524320 | tf_op jit(solution)/shard_map/ppermute | solution.py:145
  53.9 1.2 %project.1 = (f32[8,56,512]{2,1,0:T(8,128)S(1)}, bf16[512,512]{1,0:T(8,128)(2,1)S(1)}, bf16[512,512]{1,0:T(8,128)(2,1)S(1)}) custom-call(s32[1]{0:T(128)} %bitcast.core_ref, f32[2,2,2,4,8,512]{5,4,3,2,1,0:T(8,128)S(1)} %bitcast.14, f32[2,2,2,4,8,512]{5,4,3,2,1,0:T(8,128)S(1)} %collective-permute-done.other_ref, ...), custom_call_target="tpu_custom_call" | custom-call | tf_op jit(solution)/shard_map/project/pallas_call | solution.py:102
  55.1 19.7 %all_to_all.16 = f32[8,56,512]{2,1,0:T(8,128)S(1)} all-to-all(f32[8,56,512]{2,1,0:T(8,128)S(1)} %get-tuple-element.13), channel_id=1, replica_groups=mesh['x'=4,'pair'=2,'near'=2,'yfar'=2,'ymid'=2,'ynear'=2,'zh'=4,'core'=2..., dimensions={0} | all-to-all | bytes 1835008 | tf_op jit(solution)/shard_map/all_to_all | solution.py:133
  74.8 0.1 reduce_sum.18
  74.8 7.7 %all-gather.1 = f32[112,512]{1,0:T(8,128)S(1)} all-gather(f32[56,512]{1,0:T(8,128)S(1)} %reduce_sum.18), channel_id=3, replica_groups=mesh['x'=4,'pair'=2,'near'=2,'yfar'=2,'ymid'=2,'ynear'=2,'zh'=4,'core'=2..., dimensions={0}, use_global_device_ids=true | all-gather | bytes 344064 | tf_op jit(solution)/shard_map/all_gather | solution.py:151
  82.6 0.0 copy-start.2
  82.6 0.1 broadcast_in_dim.5
  82.7 0.0 copy-start
  82.7 0.0 copy-start.1
  82.7 16.2 %all_to_all.17.low_ref = f32[8,56,512]{2,1,0:T(8,128)S(1)} all-to-all(f32[8,56,512]{2,1,0:T(8,128)S(1)} %broadcast_in_dim.5), channel_id=1, replica_groups=mesh['x'=4,'pair'=2,'near'=2,'yfar'=2,'ymid'=2,'ynear'=2,'zh'=4,'core'=2..., dimensions={0} | all-to-all | bytes 1835008 | tf_op jit(solution)/shard_map/all_to_all | solution.py:133
  98.9 0.0 copy-done.2
  98.9 0.0 copy-done
  98.9 0.0 copy-done.1
  98.9 2.1 %step.1 = (f32[448,512]{1,0:T(8,128)}, f32[448,512]{1,0:T(8,128)}, f32[448,512]{1,0:T(8,128)}) custom-call(f32[8,56,512]{2,1,0:T(8,128)S(1)} %all_to_all.17.low_ref, f32[448,512]{1,0:T(8,128)S(1)} %bitcast.15, f32[448,512]{1,0:T(8,128)S(1)} %bitcast.16, f32[448,512]{1,0:T(8,128)S(1)} %bitcast.17, bf16[512,512]{1,0:T(8,128)(2,1)S(1)} %get-tuple-element.14.high_ref, ...), custom_call_target="tpu_custom_call" | custom-call | tf_op jit(solution)/shard_map/step/pallas_call | solution.py:121
  (2 shorter events, 0.1 us)
Async XLA Ops:
  0.6 51.4 %copy-start.3 = (f32[512,448]{0,1:T(8,128)S(1)}, f32[512,448]{0,1:T(8,128)}, u32[]{:S(2)}) copy-start(f32[512,448]{0,1:T(8,128)} %param.5) | copy-start | bytes 2752516
  50.1 3.8 %collective-permute-start = (f32[2,2,2,4,8,512]{5,4,3,2,1,0:T(8,128)S(1)}, f32[2,2,2,4,8,512]{5,4,3,2,1,0:T(8,128)S(1)}, u32[]{:S(2)}, u32[]{:S(2)}) collective-permute-start(f32[2,2,2,4,8,512]{5,4,3,2,1,0:T(8,128)S(1)} %bitcast.12), channel_id=1, source_target_pairs={{0,1},{1,0},{2,3},{3,2},{4,5},{5,4},{6,7},{7,6},{8,9},{9,8},{10,11... | collective-permute-start | bytes 1572872 | tf_op jit(solution)/shard_map/ppermute | solution.py:145
  82.6 16.3 %copy-start.2 = (f32[512,448]{0,1:T(8,128)S(1)}, f32[512,448]{0,1:T(8,128)}, u32[]{:S(2)}) copy-start(f32[512,448]{0,1:T(8,128)} %param.6) | copy-start | bytes 2752516
  82.7 16.2 %copy-start = (f32[512,448]{0,1:T(8,128)S(1)}, f32[512,448]{0,1:T(8,128)}, u32[]{:S(2)}) copy-start(f32[512,448]{0,1:T(8,128)} %param.8) | copy-start | bytes 2752516
  82.7 16.2 %copy-start.1 = (f32[512,448]{0,1:T(8,128)S(1)}, f32[512,448]{0,1:T(8,128)}, u32[]{:S(2)}) copy-start(f32[512,448]{0,1:T(8,128)} %param.9) | copy-start | bytes 2752516
